TPU v7x, 256 devices: a whole 4x4x8 slice. The times are simulated.
256 devices in a mesh: dp: 64 (over z, y, x_hi), mp: 4 (over x_lo, core).
Axes of the slice: x: 4 (x_hi: 2, x_lo: 2; x = x_hi * 2 + x_lo), y: 4, z: 8, core: 2. Of those that a mesh axis runs over, the one named last changes fastest.
Arguments:
- frames: bfloat16 [32768, 1024], P('dp'), may hold values from -6 to 6
- norm_gain: float32 [1024], replicated, may hold values from 0.25 to 1.75
- w_inner: bfloat16 [1024, 2048], P(None, 'mp'), may hold values from -0.1875 to 0.1875
- w_outer: bfloat16 [2048, 1024], P('mp'), may hold values from -0.125 to 0.125
- lengths: int32 [64, 8], P('dp'), may hold values from 1 to 256, 512 in all within a row
- frame_mask: int32 [32768], P('dp'), may hold values 0 or 1
- gradient: float32 [1024, 2048], P('dp', 'mp'), may hold values from -0.8 to 0.8
Outputs:
- solution: float32 [1024, 2048], P('dp', 'mp')
- residual: float32 [1024, 2048], P('dp', 'mp')
Inputs may be any that keep to these rules, and one draw needn't show every extreme that they name: Each row holds the lengths of one group's 8 utterances and sums to 512.
All inputs are finite; a program needn't handle non-finite values. No bound on the sum of `frame_mask` on one device may be relied on, other than what follows from the above.
Results may differ from a plain program's by a relative error of at most 0.017.
Values may be sent and summed in bfloat16 or wider, within the bound.
A program may use at most 64 MiB of HBM per device.

v0:
```python
import jax
import jax.numpy as jnp
from jax import lax
from jax.sharding import PartitionSpec as P

ITERS = 2


damping = 0.03


def total(values):
    return lax.psum(values, "mp")


def on_device(frames, norm_gain, w_inner, w_outer, lengths, frame_mask, gradient):
    tok_rows = frames.shape[0]
    utt_count = lengths.shape[1]
    groups = lax.axis_size("dp")
    xf = frames.astype(jnp.float32)
    mean = jnp.mean(xf, axis=1, keepdims=True)
    var = jnp.mean((xf - mean) ** 2, axis=1, keepdims=True)
    normed = (norm_gain * (xf - mean) / jnp.sqrt(var + 1e-05)).astype(jnp.bfloat16)
    pre = jnp.dot(normed, w_inner, preferred_element_type=jnp.float32)
    sig = jax.nn.sigmoid(pre)
    slope = sig * (1.0 + pre * (1.0 - sig))
    lens = lengths[0]
    ends = jnp.cumsum(lens)
    starts = ends - lens
    pos = jnp.arange(tok_rows, dtype=jnp.int32)
    inside = (pos[:, None] >= starts[None, :]) & (pos[:, None] < ends[None, :])
    inverse = 1.0 / lens.astype(jnp.float32)
    per_frame = jnp.sum(jnp.where(inside, inverse[None, :], 0.0), axis=1)
    weight = frame_mask.astype(jnp.float32) * per_frame / (utt_count * groups)
    row_count = w_inner.shape[0] // groups
    start_vec = lax.all_gather(gradient.astype(jnp.bfloat16), "dp", axis=0, tiled=True).astype(
        gradient.dtype
    )
    solution = jnp.zeros_like(start_vec)
    residual = start_vec
    direction = start_vec
    norm_now = total(jnp.stack([jnp.sum(residual * residual)]))[0]
    for step in range(ITERS):
        vb = direction.astype(jnp.bfloat16)
        curvature_q = jnp.dot(normed, vb, preferred_element_type=jnp.float32)
        hq = (0.5 * slope * curvature_q).astype(jnp.bfloat16)
        part = jnp.dot(hq, w_outer, preferred_element_type=jnp.float32)
        u = lax.psum(part.astype(jnp.bfloat16), "mp").astype(jnp.float32)
        gy = (weight[:, None] * u).astype(jnp.bfloat16)
        gh = lax.dot_general(
            gy, w_outer, (((1,), (1,)), ((), ())), preferred_element_type=jnp.float32
        )
        ga = (0.5 * slope * gh).astype(jnp.bfloat16)
        term = lax.dot_general(
            normed, ga, (((0,), (0,)), ((), ())), preferred_element_type=jnp.float32
        )
        image = lax.psum(term, "dp") + damping * direction
        alpha = norm_now / total(jnp.stack([jnp.sum(direction * image)]))[0]
        solution = solution + alpha * direction
        residual = residual - alpha * image
        norm_next = total(jnp.stack([jnp.sum(residual * residual)]))[0]
        direction = residual + norm_next / norm_now * direction
        norm_now = norm_next
    first = lax.axis_index("dp") * row_count
    solution = lax.dynamic_slice_in_dim(solution, first, row_count, 0)
    residual = lax.dynamic_slice_in_dim(residual, first, row_count, 0)
    return (solution, residual)


def solution(mesh):
    return jax.shard_map(
        on_device,
        mesh=mesh,
        in_specs=(
            P("dp", None),
            P(),
            P(None, "mp"),
            P("mp", None),
            P("dp", None),
            P("dp"),
            P("dp", "mp"),
        ),
        out_specs=(P("dp", "mp"), P("dp", "mp")),
        check_vma=False,
    )
```

profile of v0, /device:TPU:1, one launch (start us, length us, event | category | flops | bytes accessed | tf_op | source)
XLA Modules:
  0.0 1686.5 jit_solution(1537833722316469866)
XLA Ops:
  7.2 0.0 all-gather.2.cloned.1.call-start
  7.2 1.5 convert_element_type.53
  8.8 0.0 all-gather.2.cloned.1.call-update
  8.8 0.0 all-reduce.6.cloned.1.call-start
  8.8 1.5 convert_reduce_fusion
  10.4 1.6 fusion.4
  12.0 1.7 fusion.30
  13.8 112.1 %all-gather.2.cloned.1.call-done = bf16[1024,512]{1,0:T(8,128)(2,1)} async-done(((bf16[16,512]{1,0:T(8,128)(2,1)}), bf16[1024,512]{1,0:T(8,128)(2,1)}) %all-gather.2.cloned.1.call-update) | async-done | bytes 1048592 | tf_op jit(solution)/shard_map/all_gather | solution.py:36
  125.9 4.1 convolution_convert_fusion.1
  130.0 0.0 all-reduce.6.cloned.1.call-update
  130.0 0.0 all-reduce.8.cloned.1.call-start
  130.0 0.2 reduce-window.4
  130.2 0.1 select_reduce_fusion
  130.3 47.8 %all-reduce.6.cloned.1.call-done = bf16[512,1024]{1,0:T(8,128)(2,1)} async-done(((bf16[512,1024]{1,0:T(8,128)(2,1)}), bf16[512,1024]{1,0:T(8,128)(2,1)}) %all-reduce.6.cloned.1.call-update) | async-done | bytes 1048592 | tf_op jit(solution)/shard_map/psum | solution.py:48
  178.2 4.4 fusion.14
  182.6 0.0 all-reduce.10.cloned.1.call-start
  182.6 656.9 %all-reduce.8.cloned.1.call-done = f32[1024,512]{1,0:T(8,128)} async-done(((f32[1024,512]{1,0:T(8,128)}), f32[1024,512]{1,0:T(8,128)}) %all-reduce.8.cloned.1.call-update) | async-done | bytes 2097168 | tf_op jit(solution)/shard_map/psum | solution.py:57
  839.5 2.7 fusion.7
  842.3 52.1 %all-reduce = (f32[1]{0:T(128)}, f32[1]{0:T(128)}) all-reduce(f32[1]{0:T(128)} %bitcast, f32[1]{0:T(128)} %bitcast.6), channel_id=1, replica_groups=mesh['dp'=64,'mp'=4] {'mp'}, use_global_device_ids=true, to_apply=%region_1.0 | all-reduce | flops 2 | bytes 16 | tf_op jit(solution)/shard_map/psum | solution.py:13
  895.8 4.0 multiply_reduce_fusion.1
  899.8 6.5 psum.60
  907.6 3.2 fusion.8
  910.9 4.4 convolution_convert_fusion
  915.3 0.0 all-reduce.12.cloned.1.call-start
  915.3 43.7 %all-reduce.10.cloned.1.call-done = bf16[512,1024]{1,0:T(8,128)(2,1)} async-done(((bf16[512,1024]{1,0:T(8,128)(2,1)}), bf16[512,1024]{1,0:T(8,128)(2,1)}) %all-reduce.10.cloned.1.call-update) | async-done | bytes 1048592 | tf_op jit(solution)/shard_map/psum | solution.py:48
  959.0 4.4 fusion.13
  963.4 0.0 all-reduce.12.cloned.1.call-update
  963.4 1.6 convert_element_type.54
  965.0 655.3 %all-reduce.12.cloned.1.call-done = f32[1024,512]{1,0:T(8,128)} async-done(((f32[1024,512]{1,0:T(8,128)}), f32[1024,512]{1,0:T(8,128)}) %all-reduce.12.cloned.1.call-update) | async-done | bytes 2097168 | tf_op jit(solution)/shard_map/psum | solution.py:57
  1620.4 4.7 multiply_add_fusion
  1625.1 52.1 %psum.63 = f32[1]{0:T(128)} all-reduce(f32[1]{0:T(128)} %bitcast.10), channel_id=1, replica_groups=mesh['dp'=64,'mp'=4] {'mp'}, use_global_device_ids=true, to_apply=%region_15.16 | all-reduce | flops 1 | bytes 8 | tf_op jit(solution)/shard_map/psum | solution.py:13
  1678.6 1.4 dynamic-slice_subtract_fusion
  (21 shorter events, 0.1 us)
Async XLA Ops:
  7.2 118.7 %copy-start = (bf16[512,1024]{1,0:T(8,128)(2,1)S(1)}, bf16[512,1024]{1,0:T(8,128)(2,1)}, u32[]{:S(2)}) copy-start(bf16[512,1024]{1,0:T(8,128)(2,1)} %param.10) | copy-start | bytes 3145732
  7.2 4.8 copy-start.2
  7.2 4.8 copy-start.5
  7.2 118.7 %all-gather.2.cloned.1.call-start = ((), (), s32[]{:S(2)}) async-start(), calls=%async_computation | async-start | bytes 1064960 | tf_op jit(solution)/shard_map/all_gather | solution.py:36
  8.8 169.4 %all-reduce.6.cloned.1.call-start = ((), (), s32[]{:S(2)}) async-start(), calls=%async_computation.1 | async-start | bytes 2097152 | tf_op jit(solution)/shard_map/psum | solution.py:48
  8.8 3.2 copy-start.4
  13.8 116.3 %copy-start.6 = (s32[1,8]{1,0:T(1,128)S(1)}, s32[1,8]{1,0:T(1,128)}, u32[]{:S(2)}) copy-start(s32[1,8]{1,0:T(1,128)} %param.11) | copy-start | bytes 100
  13.8 116.5 %copy-start.3 = (s32[512]{0:T(512)S(1)}, s32[512]{0:T(512)}, u32[]{:S(2)}) copy-start(s32[512]{0:T(512)} %param.12) | copy-start | bytes 6148
  130.0 709.6 %all-reduce.8.cloned.1.call-start = ((), (), s32[]{:S(2)}) async-start(), calls=%async_computation.2 | async-start | bytes 4194304 | tf_op jit(solution)/shard_map/psum | solution.py:57
  182.6 657.0 %copy-start.1 = (bf16[1024,512]{1,0:T(8,128)(2,1)S(1)}, bf16[1024,512]{1,0:T(8,128)(2,1)}, u32[]{:S(2)}) copy-start(bf16[1024,512]{1,0:T(8,128)(2,1)} %all-gather.2.cloned.1.call-done) | copy-start | bytes 3145732
  182.6 776.4 %all-reduce.10.cloned.1.call-start = ((), (), s32[]{:S(2)}) async-start(), calls=%async_computation.3 | async-start | bytes 2097152 | tf_op jit(solution)/shard_map/psum | solution.py:48
  915.3 705.1 %all-reduce.12.cloned.1.call-start = ((), (), s32[]{:S(2)}) async-start(), calls=%async_computation.4 | async-start | bytes 4194304 | tf_op jit(solution)/shard_map/psum | solution.py:57
Sparse Core Ops, SparseCore 0:
  12.2 113.6 all-gather.1
  130.1 48.0 all-reduce.5
  182.7 656.7 all-reduce.7
  915.4 43.5 all-reduce.9
  963.5 656.7 all-reduce.11
where the time goes:
time: 1690 us
  waiting for transfers between devices  1520 us (90%)
  blocking collectives  111 us (7%)
  other arithmetic  22.8 us (1%)
  matrix products  18.9 us (1%)
  between operations  17.9 us (1%)
    psum x2, waiting for transfers between devices, on_device(): image = lax.psum(term, 'dp') + damping * direction  1310 us
    all_gather x1, waiting for transfers between devices, on_device(): lax.all_gather(gradient.astype(jnp.bfloat16), 'dp', axis=0, tiled=True)  112 us
    psum x3, blocking collectives, total(): return lax.psum(values, 'mp')  111 us
    psum x2, waiting for transfers between devices, on_device(): u = lax.psum(part.astype(jnp.bfloat16), 'mp').astype(jnp.float32)  91.5 us
  transfers between devices with their start and end apart: 5, of which 5 were waited for; matrix products, arithmetic and copies ran while one was open for 0% of the time, Pallas kernels for 0%

commit v1 on v0

v1 whole, which is shorter than its diff:
```python
import jax
import jax.numpy as jnp
from jax import lax
from jax.experimental import pallas as pl
from jax.experimental.pallas import tpu as pltpu
from jax.sharding import PartitionSpec as P

MESH = pl.DeviceIdType.MESH
NZ, NW, NM = 8, 8, 4
ROWS = 16
TOK, D, F, HALF = 512, 1024, 512, 512
CH = 128
NT = TOK // CH
BLK = NW * ROWS
DAMPING = 0.03
BF, F32 = jnp.bfloat16, jnp.float32
NEAR = (1, 7, 2, 6, 3, 5, 4)
FAR = (4, 3, 5, 2, 6, 1, 7, 0)


def dot(a, b):
    return jnp.dot(a, b, preferred_element_type=F32)


def fold(p):
    s = jnp.sum(p, axis=0, keepdims=True)
    return s[:, 0:128] + s[:, 128:256] + s[:, 256:384] + s[:, 384:512]


def kernel(
    frames, gain, w_inner, w_outer, lengths, mask, grad, sol, res,
    x, wi, wo, wot, normed, normed_t, hs, wcol,
    v, vd, own, give, got, half, theirs, gy, gyo, ga, term, fromw, toz, fromz, sc_own, sc_in,
    in_sem, zs_sem, zr_sem, ws_sem, wr_sem, cs_sem, cr_sem, ls_sem, lr_sem, gs_sem, gr_sem,
    ts_sem, tr_sem, us_sem, ur_sem, as_sem, ar_sem,
):
    dp, mp = lax.axis_index("dp"), lax.axis_index("mp")
    z, w = dp // NW, dp % NW
    xl, core = mp // 2, mp % 2
    sibling = (dp, xl * 2 + (1 - core))
    partner = (dp, (1 - xl) * 2 + core)

    def zpeer(k):
        return (lax.rem(z + k, NZ) * NW + w, mp)

    def wpeer(k):
        return (z * NW + lax.rem(w + k, NW), mp)

    def mpeer(k):
        return (dp, lax.rem(mp + k, NM))

    def send(src, dst, ssem, rsem, dev):
        pltpu.make_async_remote_copy(
            src_ref=src, dst_ref=dst, send_sem=ssem, recv_sem=rsem, device_id=dev, device_id_type=MESH
        ).start()

    def landed(ref, rsem, dev):
        pltpu.make_async_remote_copy(
            src_ref=ref, dst_ref=ref, send_sem=rsem, recv_sem=rsem, device_id=dev, device_id_type=MESH
        ).wait_recv()

    def sent(ref, ssem, dev):
        pltpu.make_async_remote_copy(
            src_ref=ref, dst_ref=ref, send_sem=ssem, recv_sem=ssem, device_id=dev, device_id_type=MESH
        ).wait_send()

    loads = [
        pltpu.make_async_copy(frames, x, in_sem.at[0]),
        pltpu.make_async_copy(w_inner, wi, in_sem.at[1]),
        pltpu.make_async_copy(w_outer.at[:, pl.ds(pl.multiple_of(core * HALF, HALF), HALF)], wo.at[0], in_sem.at[2]),
        pltpu.make_async_copy(w_outer.at[:, pl.ds(pl.multiple_of((1 - core) * HALF, HALF), HALF)], wo.at[1], in_sem.at[3]),
    ]
    for c in loads:
        c.start()
    v[0, z, w] = grad[...].astype(BF)

    barrier = pltpu.get_barrier_semaphore()
    for k in range(1, NZ):
        pl.semaphore_signal(barrier, inc=1, device_id=zpeer(k), device_id_type=MESH)
    for k in range(1, NW):
        pl.semaphore_signal(barrier, inc=1, device_id=wpeer(k), device_id_type=MESH)
    for k in range(1, NM):
        pl.semaphore_signal(barrier, inc=1, device_id=mpeer(k), device_id_type=MESH)
    pl.semaphore_wait(barrier, NZ + NW + NM - 3)

    def gather_pass(it, block):
        for k in range(1, NW):
            send(v.at[it, block, w], v.at[it, block, w], ws_sem.at[it], wr_sem.at[it], wpeer(k))

    def gather_start(it):
        for k in NEAR:
            send(v.at[it, z, w], v.at[it, z, w], zs_sem.at[it], zr_sem.at[it, k], zpeer(k))
        gather_pass(it, z)

    def gather_forward(it, k):
        block = lax.rem(z + NZ - k, NZ)
        landed(v.at[it, block, w], zr_sem.at[it, k], zpeer(k))
        gather_pass(it, block)

    def gather_end(it):
        landed(v.at[it, pl.ds(0, NW - 1)], wr_sem.at[it], wpeer(1))

    def scal_send(a, phase, tile):
        sc_own[a, phase] = tile
        peers = (mpeer, wpeer, zpeer)[phase]
        for k in range(1, (NM, NW, NZ)[phase]):
            send(sc_own.at[a, phase], sc_in.at[a, phase, k], as_sem.at[a, phase], ar_sem.at[a, phase], peers(k))

    def scal_take(a, phase):
        n = (NM, NW, NZ)[phase]
        landed(sc_in.at[a, phase, pl.ds(1, n - 1)], ar_sem.at[a, phase], (mpeer, wpeer, zpeer)[phase](1))
        tile = sc_own[a, phase]
        for k in range(1, n):
            tile = tile + sc_in[a, phase, k]
        return tile

    gather_start(0)

    ends, end = [], jnp.int32(0)
    starts = []
    for j in range(8):
        starts.append(end)
        end = end + lengths[0, j]
        ends.append(end)
    for t in range(NT):
        pos = lax.broadcasted_iota(jnp.int32, (CH, 128), 0) + t * CH
        per = jnp.zeros((CH, 128), F32)
        for j in range(8):
            inverse = 1.0 / jnp.full((CH, 128), lengths[0, j], jnp.int32).astype(F32)
            per = per + jnp.where((pos >= starts[j]) & (pos < ends[j]), inverse, 0.0)
        rowi = lax.broadcasted_iota(jnp.int32, (CH, 128), 0)
        coli = lax.broadcasted_iota(jnp.int32, (CH, 128), 1)
        m = jnp.broadcast_to(mask[t : t + 1, :].astype(F32), (CH, 128))
        mcol = jnp.sum(jnp.where(rowi == coli, m, 0.0), axis=1, keepdims=True)
        wcol[pl.ds(t * CH, CH), :] = jnp.broadcast_to(mcol, (CH, 128)) * per / 512.0

    def norm_chunk(t):
        rows = pl.ds(t * CH, CH)
        xf = x[rows, :].astype(F32)
        mean = jnp.mean(xf, axis=1, keepdims=True)
        xc = xf - mean
        var = jnp.mean(xc * xc, axis=1, keepdims=True)
        nf = gain[...] * xc / jnp.sqrt(var + 1e-05)
        normed[rows, :] = nf.astype(BF)
        normed_t[:, rows] = nf.T.astype(BF)

    def slope_chunk(t):
        rows = pl.ds(t * CH, CH)
        pre = dot(normed[rows, :], wi[...])
        sig = jax.nn.sigmoid(pre)
        hs[rows, :] = 0.5 * (sig * (1.0 + pre * (1.0 - sig)))

    loads[0].wait()
    for t in range(NT):
        norm_chunk(t)
    gather_forward(0, 1)
    gather_forward(0, 7)
    loads[1].wait()
    slope_chunk(0)
    gather_forward(0, 2)
    gather_forward(0, 6)
    slope_chunk(1)
    gather_forward(0, 3)
    gather_forward(0, 5)
    slope_chunk(2)
    gather_forward(0, 4)
    slope_chunk(3)
    loads[2].wait()
    loads[3].wait()
    for i in range(2):
        wot[i] = wo[i].astype(F32).T.astype(BF)
    gather_end(0)

    def tangent(it, t, mat):
        rows = pl.ds(t * CH, CH)
        q = dot(normed[rows, :], mat)
        hq = (hs[rows, :] * q).astype(BF)
        give[it, t] = dot(hq, wo[1]).astype(BF)
        send(give.at[it, t], got.at[it, t], cs_sem.at[it], cr_sem.at[it, t], sibling)
        own[t] = dot(hq, wo[0])

    def pair_sum(it, t):
        landed(got.at[it, t], cr_sem.at[it, t], sibling)
        half[it, t] = (own[t] + got[it, t].astype(F32)).astype(BF)
        send(half.at[it, t], theirs.at[it, t], ls_sem.at[it], lr_sem.at[it, t], partner)

    def weigh(it, t):
        landed(theirs.at[it, t], lr_sem.at[it, t], partner)
        u = half[it, t].astype(F32) + theirs[it, t].astype(F32)
        wc = wcol[pl.ds(t * CH, CH), :]
        wu = jnp.concatenate([wc] * 4, axis=1) * u
        gy[it, t] = wu.astype(BF)
        send(gy.at[it, t], gyo.at[it, t], gs_sem.at[it], gr_sem.at[it, t], sibling)
        return fold(wu * u)

    def pull_back(it, t):
        landed(gyo.at[it, t], gr_sem.at[it, t], sibling)
        rows = pl.ds(t * CH, CH)
        gh = dot(gy[it, t], wot[0]) + dot(gyo[it, t], wot[1])
        ga[rows, :] = (hs[rows, :] * gh).astype(BF)

    def curve(it, mat):
        tangent(it, 0, mat)
        for t in range(1, NT):
            tangent(it, t, mat)
            pair_sum(it, t - 1)
        pair_sum(it, NT - 1)
        energy = weigh(it, 0)
        for t in range(1, NT):
            energy = energy + weigh(it, t)
            pull_back(it, t - 1)
        pull_back(it, NT - 1)
        return energy

    def terms(it):
        for off in FAR:
            to = lax.rem(z + off, NZ)
            block = dot(normed_t[pl.ds(pl.multiple_of(to * BLK, BLK), BLK), :], ga[...])
            term[it, to] = block.astype(BF).reshape(NW, ROWS, F)
            for k in range(1, NW):
                send(
                    term.at[it, to, lax.rem(w + k, NW)], fromw.at[it, off, k],
                    ts_sem.at[it], tr_sem.at[it, off], wpeer(k),
                )

    def reduce_block(it, off):
        to = lax.rem(z + off, NZ)
        landed(fromw.at[it, off, pl.ds(1, NW - 1)], tr_sem.at[it, off], wpeer(1))
        total = term[it, to, w].astype(F32)
        for k in range(1, NW):
            total = total + fromw[it, off, k].astype(F32)
        if off:
            toz[it, off] = total.astype(BF)
            send(toz.at[it, off], fromz.at[it, off], us_sem.at[it], ur_sem.at[it], zpeer(off))
        return total

    def reduce_end(it, total):
        landed(fromz.at[it, pl.ds(1, NZ - 1)], ur_sem.at[it], zpeer(1))
        for k in range(1, NZ):
            total = total + fromz[it, k].astype(F32)
        return total

    g = grad[...]
    curve(0, v[0].reshape(D, F))
    terms(0)
    for off in FAR:
        total = reduce_block(0, off)
    y0 = reduce_end(0, total)

    v[1, z, w] = y0.astype(BF)
    gather_start(1)
    pad = jnp.zeros((5, 128), F32)
    scal_send(0, 0, jnp.concatenate([fold(g * g), fold(g * y0), fold(y0 * y0), pad], axis=0))
    gather_forward(1, 1)
    gather_forward(1, 7)
    scal_send(0, 1, scal_take(0, 0))
    gather_forward(1, 2)
    gather_forward(1, 6)
    scal_send(0, 2, scal_take(0, 1))
    gather_forward(1, 3)
    gather_forward(1, 5)
    gather_forward(1, 4)
    sums = jnp.sum(scal_take(0, 2), axis=1, keepdims=True)
    gg, gyy, yy = sums[0:1], sums[1:2], sums[2:3]
    alpha0 = gg / (gyy + DAMPING * gg)
    keep = 1.0 - DAMPING * alpha0
    beta = (keep * keep * gg - 2.0 * keep * alpha0 * gyy + alpha0 * alpha0 * yy) / gg
    r1 = g - alpha0 * (y0 + DAMPING * g)
    d1 = r1 + beta * g
    gather_end(1)
    for i in range(NZ):
        g_all = v[0, i].reshape(BLK, F).astype(F32)
        y_all = v[1, i].reshape(BLK, F).astype(F32)
        vd[pl.ds(i * BLK, BLK), :] = ((keep + beta) * g_all - alpha0 * y_all).astype(BF)

    energy = curve(1, vd[...])
    curvature = 0.5 * energy + DAMPING * fold(d1 * d1)
    scal_send(1, 0, jnp.concatenate([curvature, fold(r1 * r1), jnp.zeros((6, 128), F32)], axis=0))
    terms(1)
    scal_send(1, 1, scal_take(1, 0))
    for off in FAR[:4]:
        reduce_block(1, off)
    scal_send(1, 2, scal_take(1, 1))
    for off in FAR[4:]:
        total = reduce_block(1, off)
    ad1 = reduce_end(1, total)
    sums = jnp.sum(scal_take(1, 2), axis=1, keepdims=True)
    alpha1 = sums[1:2] / sums[0:1]
    sol[...] = alpha0 * g + alpha1 * d1
    res[...] = r1 - alpha1 * (ad1 + DAMPING * d1)

    for it in range(2):
        sent(v.at[it, 0, pl.ds(0, NZ - 1)], zs_sem.at[it], zpeer(1))
        sent(v.at[it, pl.ds(0, NW - 1)], ws_sem.at[it], wpeer(1))
        sent(give.at[it], cs_sem.at[it], sibling)
        sent(half.at[it], ls_sem.at[it], partner)
        sent(gy.at[it], gs_sem.at[it], sibling)
        sent(term.at[it, pl.ds(0, NW - 1)], ts_sem.at[it], wpeer(1))
        sent(toz.at[it, pl.ds(1, NZ - 1)], us_sem.at[it], zpeer(1))
        for phase, n in enumerate((NM, NW, NZ)):
            sent(sc_in.at[it, phase, pl.ds(1, n - 1)], as_sem.at[it, phase], mpeer(1))


def on_device(frames, norm_gain, w_inner, w_outer, lengths, frame_mask, gradient):
    hbm = pl.BlockSpec(memory_space=pl.ANY)
    vmem = pl.BlockSpec(memory_space=pltpu.VMEM)
    smem = pl.BlockSpec(memory_space=pltpu.SMEM)
    dma = pltpu.SemaphoreType.DMA
    out = jax.ShapeDtypeStruct((ROWS, F), F32)
    return tuple(
        pl.pallas_call(
            kernel,
            out_shape=(out, out),
            in_specs=[hbm, vmem, hbm, hbm, smem, vmem, vmem],
            out_specs=(vmem, vmem),
            scratch_shapes=[
                pltpu.VMEM((TOK, D), BF),
                pltpu.VMEM((D, F), BF),
                pltpu.VMEM((2, F, HALF), BF),
                pltpu.VMEM((2, HALF, F), BF),
                pltpu.VMEM((TOK, D), BF),
                pltpu.VMEM((D, TOK), BF),
                pltpu.VMEM((TOK, F), F32),
                pltpu.VMEM((TOK, 128), F32),
                pltpu.VMEM((2, NZ, NW, ROWS, F), BF),
                pltpu.VMEM((D, F), BF),
                pltpu.VMEM((NT, CH, HALF), F32),
                pltpu.VMEM((2, NT, CH, HALF), BF),
                pltpu.VMEM((2, NT, CH, HALF), BF),
                pltpu.VMEM((2, NT, CH, HALF), BF),
                pltpu.VMEM((2, NT, CH, HALF), BF),
                pltpu.VMEM((2, NT, CH, HALF), BF),
                pltpu.VMEM((2, NT, CH, HALF), BF),
                pltpu.VMEM((TOK, F), BF),
                pltpu.VMEM((2, NZ, NW, ROWS, F), BF),
                pltpu.VMEM((2, NZ, NW, ROWS, F), BF),
                pltpu.VMEM((2, NZ, ROWS, F), BF),
                pltpu.VMEM((2, NZ, ROWS, F), BF),
                pltpu.VMEM((2, 3, 8, 128), F32),
                pltpu.VMEM((2, 3, 8, 8, 128), F32),
                dma((4,)),
                dma((2,)), dma((2, NZ)),
                dma((2,)), dma((2,)),
                dma((2,)), dma((2, NT)),
                dma((2,)), dma((2, NT)),
                dma((2,)), dma((2, NT)),
                dma((2,)), dma((2, NZ)),
                dma((2,)), dma((2,)),
                dma((2, 3)), dma((2, 3)),
            ],
            compiler_params=pltpu.CompilerParams(
                collective_id=0, has_side_effects=True, vmem_limit_bytes=48 << 20
            ),
            cost_estimate=pl.CostEstimate(flops=9 * 2 * TOK * D * F, bytes_accessed=4 << 20, transcendentals=TOK * F),
        )(
            frames, norm_gain.reshape(1, D), w_inner, w_outer, lengths, frame_mask.reshape(NT, CH), gradient,
        )
    )


def solution(mesh):
    return jax.shard_map(
        on_device,
        mesh=mesh,
        in_specs=(
            P("dp", None),
            P(),
            P(None, "mp"),
            P("mp", None),
            P("dp", None),
            P("dp"),
            P("dp", "mp"),
        ),
        out_specs=(P("dp", "mp"), P("dp", "mp")),
        check_vma=False,
    )
```

time: 1690 us -> 123 us (0.07)
  waiting for transfers between devices: 1520 us -> 0 us
  Pallas kernels: 0 us -> 115 us
  blocking collectives: 111 us -> 0 us
  other arithmetic: 22.8 us -> 0 us
  matrix products: 18.9 us -> 0 us
  between operations: 17.9 us -> 0.66 us
    psum x4 -> x0, waiting for transfers between devices: 1400 us -> none  [the longest x2 1310 us: on_device(): image = lax.psum(term, 'dp') + damping * direction]
    pallas_call x0 -> x1, Pallas kernels: none -> 115 us  [on_device(): pl.pallas_call(kernel, out_shape=(out, out), in_specs=[hbm, vmem, hbm, hb...]
    all_gather x1 -> x0, waiting for transfers between devices: 112 us -> none  [on_device(): lax.all_gather(gradient.astype(jnp.bfloat16), 'dp', axis=0, tiled=True)]
    psum x3 -> x0, blocking collectives: 111 us -> none  [total(): return lax.psum(values, 'mp')]
    dot_general x5 -> x0, matrix products: 18.9 us -> none  [the longest x2 8.76 us: on_device(): lax.dot_general(normed, ga, (((0,), (0,)), ((), ())), preferred_element_t...]
  transfers between devices with their start and end apart: 5 -> 0, of which waited for: 5 -> 0; matrix products, arithmetic and copies ran while one was open for 0% -> 0% of each run, Pallas kernels for 0% -> 0%
where the time goes in v1:
time: 123 us
  Pallas kernels  115 us (93%)
  local copies, waits for them, and re-layouts  7.02 us (6%)
    pallas_call x1, Pallas kernels, on_device(): pl.pallas_call(kernel, out_shape=(out, out), in_specs=[hbm, vmem, hbm, hb...  115 us
    unnamed x16, local copies, waits for them, and re-layouts  7.02 us

profile of v1, /device:TPU:1, one launch (start us, length us, event | category | flops | bytes accessed | tf_op | source)
XLA Modules:
  0.0 123.0 jit_solution(3760431932565906757)
XLA Ops:
  0.6 0.0 copy-start.5
  0.6 0.0 copy-start.6
  0.7 0.7 copy-done.5
  1.3 0.0 copy-done.6
  1.3 0.0 copy-start
  1.3 1.2 copy-done
  2.5 0.0 copy-start.1
  2.5 1.2 copy-done.1
  3.8 0.0 copy-start.2
  3.8 1.2 copy-done.2
  5.0 0.0 copy-start.3
  5.0 0.8 copy-done.3
  5.8 0.0 copy-start.4
  5.8 0.7 copy-done.4
  6.4 115.3 %shard_map.86 = (f32[16,512]{1,0:T(8,128)S(1)}, f32[16,512]{1,0:T(8,128)S(1)}) custom-call(bf16[512,1024]{1,0:T(8,128)(2,1)S(1)} %copy-done, f32[1,1024]{1,0:T(1,128)S(1)} %bitcast.2, bf16[1024,512]{1,0:T(8,128)(2,1)S(1)} %copy-done.1, bf16[512,1024]{1,0:T(8,128)(2,1)S(1)} %copy-done.2, s32[1,8]{1,0:T(1,128)S(1)} %copy-done.6, s32[4,128]{1,0:T(4,128)S(1)} %bitcast.3, ...), custom_call_target="tpu_custom_call" | custom-call | flops 4831838208 | bytes 4194304 | tf_op jit(solution)/shard_map/pallas_call | solution.py:311
  121.8 0.6 copy.11
  122.4 0.6 copy.12
Async XLA Ops:
  0.6 0.7 copy-start.5
  0.6 0.7 copy-start.6
  1.3 1.2 copy-start
  2.5 1.2 copy-start.1
  3.8 1.2 copy-start.2
  5.0 0.8 copy-start.3
  5.8 0.7 copy-start.4

commit v2 on v1

--- a/solution.py
+++ b/solution.py
@@ -28,8 +28,8 @@
 
 
 def kernel(
-    frames, gain, w_inner, w_outer, lengths, mask, grad, sol, res,
-    x, wi, wo, wot, normed, normed_t, hs, wcol,
+    frames, gain_in, w_inner, w_outer, lengths, mask_in, grad_in, sol, res,
+    grad, gain, mask, x, wi, wo, wot, normed, normed_t, hs, wcol,
     v, vd, own, give, got, half, theirs, gy, gyo, ga, term, fromw, toz, fromz, sc_own, sc_in,
     in_sem, zs_sem, zr_sem, ws_sem, wr_sem, cs_sem, cr_sem, ls_sem, lr_sem, gs_sem, gr_sem,
     ts_sem, tr_sem, us_sem, ur_sem, as_sem, ar_sem,
@@ -64,6 +64,13 @@
             src_ref=ref, dst_ref=ref, send_sem=ssem, recv_sem=ssem, device_id=dev, device_id_type=MESH
         ).wait_send()
 
+    small = [
+        pltpu.make_async_copy(grad_in, grad, in_sem.at[4]),
+        pltpu.make_async_copy(gain_in, gain, in_sem.at[5]),
+        pltpu.make_async_copy(mask_in, mask, in_sem.at[6]),
+    ]
+    for c in small:
+        c.start()
     loads = [
         pltpu.make_async_copy(frames, x, in_sem.at[0]),
         pltpu.make_async_copy(w_inner, wi, in_sem.at[1]),
@@ -72,8 +79,6 @@
     ]
     for c in loads:
         c.start()
-    v[0, z, w] = grad[...].astype(BF)
-
     barrier = pltpu.get_barrier_semaphore()
     for k in range(1, NZ):
         pl.semaphore_signal(barrier, inc=1, device_id=zpeer(k), device_id_type=MESH)
@@ -81,6 +86,9 @@
         pl.semaphore_signal(barrier, inc=1, device_id=wpeer(k), device_id_type=MESH)
     for k in range(1, NM):
         pl.semaphore_signal(barrier, inc=1, device_id=mpeer(k), device_id_type=MESH)
+    for c in small:
+        c.wait()
+    v[0, z, w] = grad[...].astype(BF)
     pl.semaphore_wait(barrier, NZ + NW + NM - 3)
 
     def gather_pass(it, block):
@@ -100,15 +108,17 @@
     def gather_end(it):
         landed(v.at[it, pl.ds(0, NW - 1)], wr_sem.at[it], wpeer(1))
 
-    def scal_send(a, phase, tile):
+    peers_of = (mpeer, wpeer, zpeer, lambda k: sibling)
+    count_of = (NM, NW, NZ, 2)
+
+    def scal_send(a, phase, kind, tile):
         sc_own[a, phase] = tile
-        peers = (mpeer, wpeer, zpeer)[phase]
-        for k in range(1, (NM, NW, NZ)[phase]):
-            send(sc_own.at[a, phase], sc_in.at[a, phase, k], as_sem.at[a, phase], ar_sem.at[a, phase], peers(k))
-
-    def scal_take(a, phase):
-        n = (NM, NW, NZ)[phase]
-        landed(sc_in.at[a, phase, pl.ds(1, n - 1)], ar_sem.at[a, phase], (mpeer, wpeer, zpeer)[phase](1))
+        for k in range(1, count_of[kind]):
+            send(sc_own.at[a, phase], sc_in.at[a, phase, k], as_sem.at[a, phase], ar_sem.at[a, phase], peers_of[kind](k))
+
+    def scal_take(a, phase, kind):
+        n = count_of[kind]
+        landed(sc_in.at[a, phase, pl.ds(1, n - 1)], ar_sem.at[a, phase], peers_of[kind](1))
         tile = sc_own[a, phase]
         for k in range(1, n):
             tile = tile + sc_in[a, phase, k]
@@ -199,18 +209,21 @@
         gh = dot(gy[it, t], wot[0]) + dot(gyo[it, t], wot[1])
         ga[rows, :] = (hs[rows, :] * gh).astype(BF)
 
-    def curve(it, mat):
+    def curve(it, mat, hook0, hook1, hook2):
         tangent(it, 0, mat)
         for t in range(1, NT):
             tangent(it, t, mat)
             pair_sum(it, t - 1)
         pair_sum(it, NT - 1)
+        hook0()
         energy = weigh(it, 0)
         for t in range(1, NT):
             energy = energy + weigh(it, t)
             pull_back(it, t - 1)
+            if t == 1:
+                hook1()
+        hook2(energy)
         pull_back(it, NT - 1)
-        return energy
 
     def terms(it):
         for off in FAR:
@@ -241,26 +254,26 @@
         return total
 
     g = grad[...]
-    curve(0, v[0].reshape(D, F))
+    curve(0, v[0].reshape(D, F), lambda: None, lambda: None, lambda energy: None)
     terms(0)
     for off in FAR:
         total = reduce_block(0, off)
     y0 = reduce_end(0, total)
 
     v[1, z, w] = y0.astype(BF)
+    pad = jnp.zeros((5, 128), F32)
+    scal_send(0, 0, 0, jnp.concatenate([fold(g * g), fold(g * y0), fold(y0 * y0), pad], axis=0))
     gather_start(1)
-    pad = jnp.zeros((5, 128), F32)
-    scal_send(0, 0, jnp.concatenate([fold(g * g), fold(g * y0), fold(y0 * y0), pad], axis=0))
+    scal_send(0, 1, 1, scal_take(0, 0, 0))
     gather_forward(1, 1)
     gather_forward(1, 7)
-    scal_send(0, 1, scal_take(0, 0))
     gather_forward(1, 2)
     gather_forward(1, 6)
-    scal_send(0, 2, scal_take(0, 1))
     gather_forward(1, 3)
     gather_forward(1, 5)
     gather_forward(1, 4)
-    sums = jnp.sum(scal_take(0, 2), axis=1, keepdims=True)
+    scal_send(0, 2, 2, scal_take(0, 1, 1))
+    sums = jnp.sum(scal_take(0, 2, 2), axis=1, keepdims=True)
     gg, gyy, yy = sums[0:1], sums[1:2], sums[2:3]
     alpha0 = gg / (gyy + DAMPING * gg)
     keep = 1.0 - DAMPING * alpha0
@@ -273,19 +286,27 @@
         y_all = v[1, i].reshape(BLK, F).astype(F32)
         vd[pl.ds(i * BLK, BLK), :] = ((keep + beta) * g_all - alpha0 * y_all).astype(BF)
 
-    energy = curve(1, vd[...])
-    curvature = 0.5 * energy + DAMPING * fold(d1 * d1)
-    scal_send(1, 0, jnp.concatenate([curvature, fold(r1 * r1), jnp.zeros((6, 128), F32)], axis=0))
+    scal_send(1, 0, 0, jnp.concatenate([fold(d1 * d1), fold(r1 * r1), jnp.zeros((6, 128), F32)], axis=0))
+
+    def first_hop():
+        scal_send(1, 1, 1, scal_take(1, 0, 0))
+
+    def second_hop():
+        scal_send(1, 2, 2, scal_take(1, 1, 1))
+
+    def last_hop(energy):
+        scal_send(2, 0, 3, jnp.broadcast_to(energy, (8, 128)))
+
+    curve(1, vd[...], first_hop, second_hop, last_hop)
+    scal_send(2, 1, 1, scal_take(2, 0, 3))
     terms(1)
-    scal_send(1, 1, scal_take(1, 0))
-    for off in FAR[:4]:
-        reduce_block(1, off)
-    scal_send(1, 2, scal_take(1, 1))
-    for off in FAR[4:]:
+    norms = jnp.sum(scal_take(1, 2, 2), axis=1, keepdims=True)
+    scal_send(2, 2, 2, scal_take(2, 1, 1))
+    for off in FAR:
         total = reduce_block(1, off)
     ad1 = reduce_end(1, total)
-    sums = jnp.sum(scal_take(1, 2), axis=1, keepdims=True)
-    alpha1 = sums[1:2] / sums[0:1]
+    energy = jnp.sum(scal_take(2, 2, 2)[0:1], axis=1, keepdims=True)
+    alpha1 = norms[1:2] / (energy + DAMPING * norms[0:1])
     sol[...] = alpha0 * g + alpha1 * d1
     res[...] = r1 - alpha1 * (ad1 + DAMPING * d1)
 
@@ -297,8 +318,9 @@
         sent(gy.at[it], gs_sem.at[it], sibling)
         sent(term.at[it, pl.ds(0, NW - 1)], ts_sem.at[it], wpeer(1))
         sent(toz.at[it, pl.ds(1, NZ - 1)], us_sem.at[it], zpeer(1))
-        for phase, n in enumerate((NM, NW, NZ)):
-            sent(sc_in.at[it, phase, pl.ds(1, n - 1)], as_sem.at[it, phase], mpeer(1))
+    for a in range(3):
+        for phase, n in enumerate((2 if a == 2 else NM, NW, NZ)):
+            sent(sc_in.at[a, phase, pl.ds(1, n - 1)], as_sem.at[a, phase], mpeer(1))
 
 
 def on_device(frames, norm_gain, w_inner, w_outer, lengths, frame_mask, gradient):
@@ -311,9 +333,12 @@
         pl.pallas_call(
             kernel,
             out_shape=(out, out),
-            in_specs=[hbm, vmem, hbm, hbm, smem, vmem, vmem],
+            in_specs=[hbm, hbm, hbm, hbm, smem, hbm, hbm],
             out_specs=(vmem, vmem),
             scratch_shapes=[
+                pltpu.VMEM((ROWS, F), F32),
+                pltpu.VMEM((1, D), F32),
+                pltpu.VMEM((NT, CH), jnp.int32),
                 pltpu.VMEM((TOK, D), BF),
                 pltpu.VMEM((D, F), BF),
                 pltpu.VMEM((2, F, HALF), BF),
@@ -336,9 +361,9 @@
                 pltpu.VMEM((2, NZ, NW, ROWS, F), BF),
                 pltpu.VMEM((2, NZ, ROWS, F), BF),
                 pltpu.VMEM((2, NZ, ROWS, F), BF),
-                pltpu.VMEM((2, 3, 8, 128), F32),
-                pltpu.VMEM((2, 3, 8, 8, 128), F32),
-                dma((4,)),
+                pltpu.VMEM((3, 3, 8, 128), F32),
+                pltpu.VMEM((3, 3, 8, 8, 128), F32),
+                dma((7,)),
                 dma((2,)), dma((2, NZ)),
                 dma((2,)), dma((2,)),
                 dma((2,)), dma((2, NT)),
@@ -346,10 +371,10 @@
                 dma((2,)), dma((2, NT)),
                 dma((2,)), dma((2, NZ)),
                 dma((2,)), dma((2,)),
-                dma((2, 3)), dma((2, 3)),
+                dma((3, 3)), dma((3, 3)),
             ],
             compiler_params=pltpu.CompilerParams(
-                collective_id=0, has_side_effects=True, vmem_limit_bytes=48 << 20
+                collective_id=0, has_side_effects=True, vmem_limit_bytes=63 << 20
             ),
             cost_estimate=pl.CostEstimate(flops=9 * 2 * TOK * D * F, bytes_accessed=4 << 20, transcendentals=TOK * F),
         )(

time: 123 us -> 116 us (0.943)
  local copies, waits for them, and re-layouts: 7.02 us -> 2 us
  Pallas kernels: 115 us -> 113 us
    unnamed x16 -> x4, local copies, waits for them, and re-layouts: 7.02 us -> 2 us
    pallas_call x1, Pallas kernels: 115 us -> 113 us  [on_device(): pl.pallas_call(kernel, out_shape=(out, out), in_specs=[hbm, hbm, hbm, hbm...]
where the time goes in v2:
time: 116 us
  Pallas kernels  113 us (97%)
  local copies, waits for them, and re-layouts  2 us (2%)
    pallas_call x1, Pallas kernels, on_device(): pl.pallas_call(kernel, out_shape=(out, out), in_specs=[hbm, hbm, hbm, hbm...  113 us

profile of v2, /device:TPU:1, one launch (start us, length us, event | category | flops | bytes accessed | tf_op | source)
XLA Modules:
  0.0 115.9 jit_solution(2881589615352966274)
XLA Ops:
  0.6 113.2 %shard_map.86 = (f32[16,512]{1,0:T(8,128)}, f32[16,512]{1,0:T(8,128)}) custom-call(bf16[512,1024]{1,0:T(8,128)(2,1)} %frames.1, f32[1,1024]{1,0:T(1,128)} %bitcast.2, bf16[1024,512]{1,0:T(8,128)(2,1)} %w_inner.1, bf16[512,1024]{1,0:T(8,128)(2,1)} %w_outer.1, s32[1,8]{1,0:T(1,128)} %lengths.1, s32[4,128]{1,0:T(4,128)} %bitcast.3, f32[16,512]{1,0:T(8,128)} %grad_in.1), custom_call_target="tpu_custom_call" | custom-call | flops 4831838208 | bytes 4194304 | tf_op jit(solution)/shard_map/pallas_call | solution.py:333
  113.9 0.0 copy-start
  113.9 1.4 %copy.11 = f32[16,512]{1,0:T(8,128)} copy(f32[16,512]{1,0:T(8,128)} %get-tuple-element.4) | data formatting | bytes 65536
  115.3 0.0 copy-done
  115.3 0.6 copy.12
Async XLA Ops:
  113.9 1.4 %copy-start = (f32[16,512]{1,0:T(8,128)S(1)}, f32[16,512]{1,0:T(8,128)}, u32[]{:S(2)}) copy-start(f32[16,512]{1,0:T(8,128)} %get-tuple-element.5) | copy-start | bytes 98308

commit v3 on v2

--- a/solution.py
+++ b/solution.py
@@ -10,12 +10,14 @@
 ROWS = 16
 TOK, D, F, HALF = 512, 1024, 512, 512
 CH = 128
+SHARE = CH // 2
 NT = TOK // CH
 BLK = NW * ROWS
 DAMPING = 0.03
 BF, F32 = jnp.bfloat16, jnp.float32
 NEAR = (1, 7, 2, 6, 3, 5, 4)
 FAR = (4, 3, 5, 2, 6, 1, 7, 0)
+ORDER = (0, 2, 1, 3)
 
 
 def dot(a, b):
@@ -30,15 +32,19 @@
 def kernel(
     frames, gain_in, w_inner, w_outer, lengths, mask_in, grad_in, sol, res,
     grad, gain, mask, x, wi, wo, wot, normed, normed_t, hs, wcol,
-    v, vd, own, give, got, half, theirs, gy, gyo, ga, term, fromw, toz, fromz, sc_own, sc_in,
+    wrow, v, u_first, own, give, got, half, theirs, gy, gyo, ga, term, fromw, toz, fromz, sc_own, sc_in,
     in_sem, zs_sem, zr_sem, ws_sem, wr_sem, cs_sem, cr_sem, ls_sem, lr_sem, gs_sem, gr_sem,
-    ts_sem, tr_sem, us_sem, ur_sem, as_sem, ar_sem,
+    ts_sem, tr_sem, us_sem, ur_sem, as_sem, ar_sem, xs_sem, xr_sem,
 ):
     dp, mp = lax.axis_index("dp"), lax.axis_index("mp")
     z, w = dp // NW, dp % NW
     xl, core = mp // 2, mp % 2
     sibling = (dp, xl * 2 + (1 - core))
-    partner = (dp, (1 - xl) * 2 + core)
+    xh = w % 2
+    beside = (dp, (1 - xl) * 2 + core)
+    across = (dp + 1 - 2 * xh, (1 - xl) * 2 + core)
+    kept, taken = 2 + xl, 3 - xl
+    kept_from = 2 + (xh + xl) % 2
 
     def zpeer(k):
         return (lax.rem(z + k, NZ) * NW + w, mp)
@@ -71,8 +77,15 @@
     ]
     for c in small:
         c.start()
+    def chunk(t):
+        return pl.ds(pl.multiple_of(t * CH, CH), CH)
+
+    def share(t, c):
+        return pl.ds(pl.multiple_of(t * CH + c * SHARE, SHARE), SHARE)
+
     loads = [
-        pltpu.make_async_copy(frames, x, in_sem.at[0]),
+        pltpu.make_async_copy(frames.at[pl.ds(0, 2 * CH)], x.at[pl.ds(0, 2 * CH)], in_sem.at[0]),
+        pltpu.make_async_copy(frames.at[chunk(kept_from)], x.at[chunk(kept)], in_sem.at[7]),
         pltpu.make_async_copy(w_inner, wi, in_sem.at[1]),
         pltpu.make_async_copy(w_outer.at[:, pl.ds(pl.multiple_of(core * HALF, HALF), HALF)], wo.at[0], in_sem.at[2]),
         pltpu.make_async_copy(w_outer.at[:, pl.ds(pl.multiple_of((1 - core) * HALF, HALF), HALF)], wo.at[1], in_sem.at[3]),
@@ -86,10 +99,11 @@
         pl.semaphore_signal(barrier, inc=1, device_id=wpeer(k), device_id_type=MESH)
     for k in range(1, NM):
         pl.semaphore_signal(barrier, inc=1, device_id=mpeer(k), device_id_type=MESH)
+    pl.semaphore_signal(barrier, inc=1, device_id=across, device_id_type=MESH)
     for c in small:
         c.wait()
     v[0, z, w] = grad[...].astype(BF)
-    pl.semaphore_wait(barrier, NZ + NW + NM - 3)
+    pl.semaphore_wait(barrier, NZ + NW + NM - 2)
 
     def gather_pass(it, block):
         for k in range(1, NW):
@@ -124,7 +138,13 @@
             tile = tile + sc_in[a, phase, k]
         return tile
 
+    g = grad[...]
+    scal_send(0, 0, 0, jnp.broadcast_to(fold(g * g), (8, 128)))
     gather_start(0)
+
+    send(
+        frames.at[share(kept_from, core)], x.at[share(kept, core)], xs_sem.at[0], xr_sem.at[0], across
+    )
 
     ends, end = [], jnp.int32(0)
     starts = []
@@ -132,20 +152,29 @@
         starts.append(end)
         end = end + lengths[0, j]
         ends.append(end)
-    for t in range(NT):
-        pos = lax.broadcasted_iota(jnp.int32, (CH, 128), 0) + t * CH
-        per = jnp.zeros((CH, 128), F32)
+
+    def weight_row(t):
+        pos = lax.broadcasted_iota(jnp.int32, (8, 128), 1) + t * CH
+        per = jnp.zeros((8, 128), F32)
         for j in range(8):
-            inverse = 1.0 / jnp.full((CH, 128), lengths[0, j], jnp.int32).astype(F32)
+            inverse = 1.0 / jnp.full((8, 128), lengths[0, j], jnp.int32).astype(F32)
             per = per + jnp.where((pos >= starts[j]) & (pos < ends[j]), inverse, 0.0)
+        return mask[pl.ds(t, 1), :].astype(F32) * per / 512.0
+
+    def weight_column(row):
         rowi = lax.broadcasted_iota(jnp.int32, (CH, 128), 0)
         coli = lax.broadcasted_iota(jnp.int32, (CH, 128), 1)
-        m = jnp.broadcast_to(mask[t : t + 1, :].astype(F32), (CH, 128))
-        mcol = jnp.sum(jnp.where(rowi == coli, m, 0.0), axis=1, keepdims=True)
-        wcol[pl.ds(t * CH, CH), :] = jnp.broadcast_to(mcol, (CH, 128)) * per / 512.0
+        spread = jnp.where(rowi == coli, jnp.broadcast_to(row[0:1], (CH, 128)), 0.0)
+        return jnp.broadcast_to(jnp.sum(spread, axis=1, keepdims=True), (CH, 128))
+
+    wrow[0] = weight_row(kept_from)
+    send(wrow.at[0], wrow.at[1], xs_sem.at[1], xr_sem.at[1], across)
+    for t in range(2):
+        wcol[chunk(t), :] = weight_column(weight_row(t))
+    wcol[chunk(kept), :] = weight_column(wrow[0])
 
     def norm_chunk(t):
-        rows = pl.ds(t * CH, CH)
+        rows = chunk(t)
         xf = x[rows, :].astype(F32)
         mean = jnp.mean(xf, axis=1, keepdims=True)
         xc = xf - mean
@@ -155,34 +184,44 @@
         normed_t[:, rows] = nf.T.astype(BF)
 
     def slope_chunk(t):
-        rows = pl.ds(t * CH, CH)
+        rows = chunk(t)
         pre = dot(normed[rows, :], wi[...])
         sig = jax.nn.sigmoid(pre)
         hs[rows, :] = 0.5 * (sig * (1.0 + pre * (1.0 - sig)))
 
     loads[0].wait()
-    for t in range(NT):
-        norm_chunk(t)
+    norm_chunk(0)
+    norm_chunk(1)
+    loads[1].wait()
+    norm_chunk(kept)
+    scal_send(0, 1, 1, scal_take(0, 0, 0))
     gather_forward(0, 1)
     gather_forward(0, 7)
-    loads[1].wait()
+    landed(x.at[share(taken, core)], xr_sem.at[0], across)
+    send(x.at[share(taken, core)], x.at[share(taken, core)], xs_sem.at[2], xr_sem.at[2], sibling)
+    loads[2].wait()
     slope_chunk(0)
     gather_forward(0, 2)
     gather_forward(0, 6)
     slope_chunk(1)
     gather_forward(0, 3)
     gather_forward(0, 5)
-    slope_chunk(2)
     gather_forward(0, 4)
-    slope_chunk(3)
-    loads[2].wait()
+    scal_send(0, 2, 2, scal_take(0, 1, 1))
+    slope_chunk(kept)
+    landed(wrow.at[1], xr_sem.at[1], across)
+    wcol[chunk(taken), :] = weight_column(wrow[1])
     loads[3].wait()
+    loads[4].wait()
     for i in range(2):
         wot[i] = wo[i].astype(F32).T.astype(BF)
+    landed(x.at[share(taken, 1 - core)], xr_sem.at[2], sibling)
+    norm_chunk(taken)
+    slope_chunk(taken)
     gather_end(0)
 
     def tangent(it, t, mat):
-        rows = pl.ds(t * CH, CH)
+        rows = chunk(t)
         q = dot(normed[rows, :], mat)
         hq = (hs[rows, :] * q).astype(BF)
         give[it, t] = dot(hq, wo[1]).astype(BF)
@@ -192,12 +231,16 @@
     def pair_sum(it, t):
         landed(got.at[it, t], cr_sem.at[it, t], sibling)
         half[it, t] = (own[t] + got[it, t].astype(F32)).astype(BF)
-        send(half.at[it, t], theirs.at[it, t], ls_sem.at[it], lr_sem.at[it, t], partner)
-
-    def weigh(it, t):
-        landed(theirs.at[it, t], lr_sem.at[it, t], partner)
+        send(half.at[it, t], theirs.at[it, t], ls_sem.at[it], lr_sem.at[it, t], across if t > 1 else beside)
+
+    def weigh(it, t, beta):
+        landed(theirs.at[it, t], lr_sem.at[it, t], across if t > 1 else beside)
         u = half[it, t].astype(F32) + theirs[it, t].astype(F32)
-        wc = wcol[pl.ds(t * CH, CH), :]
+        if it == 0:
+            u_first[t] = u
+        else:
+            u = u + beta * u_first[t]
+        wc = wcol[chunk(t), :]
         wu = jnp.concatenate([wc] * 4, axis=1) * u
         gy[it, t] = wu.astype(BF)
         send(gy.at[it, t], gyo.at[it, t], gs_sem.at[it], gr_sem.at[it, t], sibling)
@@ -205,25 +248,24 @@
 
     def pull_back(it, t):
         landed(gyo.at[it, t], gr_sem.at[it, t], sibling)
-        rows = pl.ds(t * CH, CH)
+        rows = chunk(t)
         gh = dot(gy[it, t], wot[0]) + dot(gyo[it, t], wot[1])
         ga[rows, :] = (hs[rows, :] * gh).astype(BF)
 
-    def curve(it, mat, hook0, hook1, hook2):
-        tangent(it, 0, mat)
-        for t in range(1, NT):
-            tangent(it, t, mat)
-            pair_sum(it, t - 1)
-        pair_sum(it, NT - 1)
-        hook0()
-        energy = weigh(it, 0)
-        for t in range(1, NT):
-            energy = energy + weigh(it, t)
-            pull_back(it, t - 1)
-            if t == 1:
-                hook1()
-        hook2(energy)
-        pull_back(it, NT - 1)
+    def curve(it, mat, get_beta):
+        tangent(it, ORDER[0], mat)
+        for i in range(1, NT):
+            tangent(it, ORDER[i], mat)
+            pair_sum(it, ORDER[i - 1])
+        pair_sum(it, ORDER[NT - 1])
+        beta = get_beta()
+        energy = weigh(it, ORDER[0], beta)
+        for i in range(1, NT):
+            energy = energy + weigh(it, ORDER[i], beta)
+            pull_back(it, ORDER[i - 1])
+        scal_send(2 * it + 1, 0, 3, jnp.broadcast_to(energy, (8, 128)))
+        pull_back(it, ORDER[NT - 1])
+        scal_send(2 * it + 1, 1, 1, scal_take(2 * it + 1, 0, 3))
 
     def terms(it):
         for off in FAR:
@@ -253,18 +295,22 @@
             total = total + fromz[it, k].astype(F32)
         return total
 
-    g = grad[...]
-    curve(0, v[0].reshape(D, F), lambda: None, lambda: None, lambda energy: None)
-    terms(0)
-    for off in FAR:
-        total = reduce_block(0, off)
-    y0 = reduce_end(0, total)
-
-    v[1, z, w] = y0.astype(BF)
-    pad = jnp.zeros((5, 128), F32)
-    scal_send(0, 0, 0, jnp.concatenate([fold(g * g), fold(g * y0), fold(y0 * y0), pad], axis=0))
+    def reduce(it):
+        terms(it)
+        scal_send(2 * it + 1, 2, 2, scal_take(2 * it + 1, 1, 1))
+        for off in FAR:
+            total = reduce_block(it, off)
+        total = reduce_end(it, total)
+        return total, jnp.sum(scal_take(2 * it + 1, 2, 2)[0:1], axis=1, keepdims=True)
+
+    curve(0, v[0].reshape(D, F), lambda: None)
+    gg = jnp.sum(scal_take(0, 2, 2)[0:1], axis=1, keepdims=True)
+    ag, energy0 = reduce(0)
+    alpha0 = gg / (energy0 + DAMPING * gg)
+    r1 = g - alpha0 * (ag + DAMPING * g)
+    v[1, z, w] = r1.astype(BF)
     gather_start(1)
-    scal_send(0, 1, 1, scal_take(0, 0, 0))
+    scal_send(2, 0, 0, jnp.concatenate([fold(r1 * r1), fold(r1 * g), jnp.zeros((6, 128), F32)], axis=0))
     gather_forward(1, 1)
     gather_forward(1, 7)
     gather_forward(1, 2)
@@ -272,41 +318,22 @@
     gather_forward(1, 3)
     gather_forward(1, 5)
     gather_forward(1, 4)
-    scal_send(0, 2, 2, scal_take(0, 1, 1))
-    sums = jnp.sum(scal_take(0, 2, 2), axis=1, keepdims=True)
-    gg, gyy, yy = sums[0:1], sums[1:2], sums[2:3]
-    alpha0 = gg / (gyy + DAMPING * gg)
-    keep = 1.0 - DAMPING * alpha0
-    beta = (keep * keep * gg - 2.0 * keep * alpha0 * gyy + alpha0 * alpha0 * yy) / gg
-    r1 = g - alpha0 * (y0 + DAMPING * g)
+    scal_send(2, 1, 1, scal_take(2, 0, 0))
+    gather_end(1)
+    scal_send(2, 2, 2, scal_take(2, 1, 1))
+
+    norms = []
+
+    def get_beta():
+        sums = jnp.sum(scal_take(2, 2, 2), axis=1, keepdims=True)
+        norms.extend([sums[0:1], sums[1:2], sums[0:1] / gg])
+        return norms[2]
+
+    curve(1, v[1].reshape(D, F), get_beta)
+    rr1, rg, beta = norms
+    ad1, energy1 = reduce(1)
     d1 = r1 + beta * g
-    gather_end(1)
-    for i in range(NZ):
-        g_all = v[0, i].reshape(BLK, F).astype(F32)
-        y_all = v[1, i].reshape(BLK, F).astype(F32)
-        vd[pl.ds(i * BLK, BLK), :] = ((keep + beta) * g_all - alpha0 * y_all).astype(BF)
-
-    scal_send(1, 0, 0, jnp.concatenate([fold(d1 * d1), fold(r1 * r1), jnp.zeros((6, 128), F32)], axis=0))
-
-    def first_hop():
-        scal_send(1, 1, 1, scal_take(1, 0, 0))
-
-    def second_hop():
-        scal_send(1, 2, 2, scal_take(1, 1, 1))
-
-    def last_hop(energy):
-        scal_send(2, 0, 3, jnp.broadcast_to(energy, (8, 128)))
-
-    curve(1, vd[...], first_hop, second_hop, last_hop)
-    scal_send(2, 1, 1, scal_take(2, 0, 3))
-    terms(1)
-    norms = jnp.sum(scal_take(1, 2, 2), axis=1, keepdims=True)
-    scal_send(2, 2, 2, scal_take(2, 1, 1))
-    for off in FAR:
-        total = reduce_block(1, off)
-    ad1 = reduce_end(1, total)
-    energy = jnp.sum(scal_take(2, 2, 2)[0:1], axis=1, keepdims=True)
-    alpha1 = norms[1:2] / (energy + DAMPING * norms[0:1])
+    alpha1 = rr1 / (energy1 + DAMPING * (rr1 + 2.0 * beta * rg + beta * beta * gg))
     sol[...] = alpha0 * g + alpha1 * d1
     res[...] = r1 - alpha1 * (ad1 + DAMPING * d1)
 
@@ -314,13 +341,16 @@
         sent(v.at[it, 0, pl.ds(0, NZ - 1)], zs_sem.at[it], zpeer(1))
         sent(v.at[it, pl.ds(0, NW - 1)], ws_sem.at[it], wpeer(1))
         sent(give.at[it], cs_sem.at[it], sibling)
-        sent(half.at[it], ls_sem.at[it], partner)
+        sent(half.at[it], ls_sem.at[it], beside)
         sent(gy.at[it], gs_sem.at[it], sibling)
         sent(term.at[it, pl.ds(0, NW - 1)], ts_sem.at[it], wpeer(1))
         sent(toz.at[it, pl.ds(1, NZ - 1)], us_sem.at[it], zpeer(1))
-    for a in range(3):
-        for phase, n in enumerate((2 if a == 2 else NM, NW, NZ)):
+    for a in range(4):
+        for phase, n in enumerate((2 if a % 2 else NM, NW, NZ)):
             sent(sc_in.at[a, phase, pl.ds(1, n - 1)], as_sem.at[a, phase], mpeer(1))
+    sent(x.at[share(kept, core)], xs_sem.at[0], across)
+    sent(wrow.at[0], xs_sem.at[1], across)
+    sent(x.at[share(taken, core)], xs_sem.at[2], sibling)
 
 
 def on_device(frames, norm_gain, w_inner, w_outer, lengths, frame_mask, gradient):
@@ -347,8 +377,9 @@
                 pltpu.VMEM((D, TOK), BF),
                 pltpu.VMEM((TOK, F), F32),
                 pltpu.VMEM((TOK, 128), F32),
+                pltpu.VMEM((2, 8, 128), F32),
                 pltpu.VMEM((2, NZ, NW, ROWS, F), BF),
-                pltpu.VMEM((D, F), BF),
+                pltpu.VMEM((NT, CH, HALF), F32),
                 pltpu.VMEM((NT, CH, HALF), F32),
                 pltpu.VMEM((2, NT, CH, HALF), BF),
                 pltpu.VMEM((2, NT, CH, HALF), BF),
@@ -361,9 +392,9 @@
                 pltpu.VMEM((2, NZ, NW, ROWS, F), BF),
                 pltpu.VMEM((2, NZ, ROWS, F), BF),
                 pltpu.VMEM((2, NZ, ROWS, F), BF),
-                pltpu.VMEM((3, 3, 8, 128), F32),
-                pltpu.VMEM((3, 3, 8, 8, 128), F32),
-                dma((7,)),
+                pltpu.VMEM((4, 3, 8, 128), F32),
+                pltpu.VMEM((4, 3, 8, 8, 128), F32),
+                dma((8,)),
                 dma((2,)), dma((2, NZ)),
                 dma((2,)), dma((2,)),
                 dma((2,)), dma((2, NT)),
@@ -371,7 +402,8 @@
                 dma((2,)), dma((2, NT)),
                 dma((2,)), dma((2, NZ)),
                 dma((2,)), dma((2,)),
-                dma((3, 3)), dma((3, 3)),
+                dma((4, 3)), dma((4, 3)),
+                dma((3,)), dma((3,)),
             ],
             compiler_params=pltpu.CompilerParams(
                 collective_id=0, has_side_effects=True, vmem_limit_bytes=63 << 20

time: 116 us -> 115 us (level)
    pallas_call x1, Pallas kernels: 113 us -> 112 us  [on_device(): pl.pallas_call(kernel, out_shape=(out, out), in_specs=[hbm, hbm, hbm, hbm...]
where the time goes in v3:
time: 115 us; the launch traced here: 114 us
  Pallas kernels  112 us (97%)
  local copies, waits for them, and re-layouts  2 us (2%)
    pallas_call x1, Pallas kernels, on_device(): pl.pallas_call(kernel, out_shape=(out, out), in_specs=[hbm, hbm, hbm, hbm...  112 us

profile of v3, /device:TPU:1, one launch (start us, length us, event | category | flops | bytes accessed | tf_op | source)
XLA Modules:
  0.0 114.3 jit_solution(9230620789438515191)
XLA Ops:
  0.6 111.7 %shard_map.86 = (f32[16,512]{1,0:T(8,128)}, f32[16,512]{1,0:T(8,128)}) custom-call(bf16[512,1024]{1,0:T(8,128)(2,1)} %frames.1, f32[1,1024]{1,0:T(1,128)} %bitcast.2, bf16[1024,512]{1,0:T(8,128)(2,1)} %w_inner.1, bf16[512,1024]{1,0:T(8,128)(2,1)} %w_outer.1, s32[1,8]{1,0:T(1,128)} %lengths.1, s32[4,128]{1,0:T(4,128)} %bitcast.3, f32[16,512]{1,0:T(8,128)} %grad_in.1), custom_call_target="tpu_custom_call" | custom-call | flops 4831838208 | bytes 4194304 | tf_op jit(solution)/shard_map/pallas_call | solution.py:363
  112.3 0.0 copy-start
  112.3 1.4 %copy.11 = f32[16,512]{1,0:T(8,128)} copy(f32[16,512]{1,0:T(8,128)} %get-tuple-element.4) | data formatting | bytes 65536
  113.7 0.0 copy-done
  113.7 0.6 copy.12
Async XLA Ops:
  112.3 1.4 %copy-start = (f32[16,512]{1,0:T(8,128)S(1)}, f32[16,512]{1,0:T(8,128)}, u32[]{:S(2)}) copy-start(f32[16,512]{1,0:T(8,128)} %get-tuple-element.5) | copy-start | bytes 98308

commit v4 on v3

--- a/solution.py
+++ b/solution.py
@@ -13,6 +13,7 @@
 SHARE = CH // 2
 NT = TOK // CH
 BLK = NW * ROWS
+CA, CB = 384, 128
 DAMPING = 0.03
 BF, F32 = jnp.bfloat16, jnp.float32
 NEAR = (1, 7, 2, 6, 3, 5, 4)
@@ -32,9 +33,9 @@
 def kernel(
     frames, gain_in, w_inner, w_outer, lengths, mask_in, grad_in, sol, res,
     grad, gain, mask, x, wi, wo, wot, normed, normed_t, hs, wcol,
-    wrow, v, u_first, own, give, got, half, theirs, gy, gyo, ga, term, fromw, toz, fromz, sc_own, sc_in,
+    wrow, va, vb, u_first, own, give, got, half, theirs, gy, gyo, ga, ta, tb, fromw, toz, fromz, bz, tow, bw, sc_own, sc_in,
     in_sem, zs_sem, zr_sem, ws_sem, wr_sem, cs_sem, cr_sem, ls_sem, lr_sem, gs_sem, gr_sem,
-    ts_sem, tr_sem, us_sem, ur_sem, as_sem, ar_sem, xs_sem, xr_sem,
+    ts_sem, tr_sem, us_sem, ur_sem, as_sem, ar_sem, xs_sem, xr_sem, bs_sem, br_sem, cbs_sem, cbr_sem,
 ):
     dp, mp = lax.axis_index("dp"), lax.axis_index("mp")
     z, w = dp // NW, dp % NW
@@ -102,25 +103,34 @@
     pl.semaphore_signal(barrier, inc=1, device_id=across, device_id_type=MESH)
     for c in small:
         c.wait()
-    v[0, z, w] = grad[...].astype(BF)
     pl.semaphore_wait(barrier, NZ + NW + NM - 2)
 
     def gather_pass(it, block):
         for k in range(1, NW):
-            send(v.at[it, block, w], v.at[it, block, w], ws_sem.at[it], wr_sem.at[it], wpeer(k))
-
-    def gather_start(it):
+            send(va.at[it, block, w], va.at[it, block, w], ws_sem.at[it], wr_sem.at[it], wpeer(k))
+
+    def gather_start(it, rows):
+        va[it, z, w] = rows[:, :CA]
+        vb[it, z, w] = rows[:, CA:]
         for k in NEAR:
-            send(v.at[it, z, w], v.at[it, z, w], zs_sem.at[it], zr_sem.at[it, k], zpeer(k))
+            send(va.at[it, z, w], va.at[it, z, w], zs_sem.at[it], zr_sem.at[it, k], zpeer(k))
+        for k in range(1, NW):
+            send(vb.at[it, z, w], vb.at[it, z, w], bs_sem.at[it, 0], br_sem.at[it, 0], wpeer(k))
         gather_pass(it, z)
 
     def gather_forward(it, k):
         block = lax.rem(z + NZ - k, NZ)
-        landed(v.at[it, block, w], zr_sem.at[it, k], zpeer(k))
+        landed(va.at[it, block, w], zr_sem.at[it, k], zpeer(k))
         gather_pass(it, block)
 
+    def gather_turn(it):
+        landed(vb.at[it, 0, pl.ds(0, NW - 1)], br_sem.at[it, 0], wpeer(1))
+        for k in NEAR[::-1]:
+            send(vb.at[it, z], vb.at[it, z], bs_sem.at[it, 1], br_sem.at[it, 1], zpeer(k))
+
     def gather_end(it):
-        landed(v.at[it, pl.ds(0, NW - 1)], wr_sem.at[it], wpeer(1))
+        landed(va.at[it, pl.ds(0, NW - 1)], wr_sem.at[it], wpeer(1))
+        landed(vb.at[it, pl.ds(0, NZ - 1)], br_sem.at[it, 1], zpeer(1))
 
     peers_of = (mpeer, wpeer, zpeer, lambda k: sibling)
     count_of = (NM, NW, NZ, 2)
@@ -140,7 +150,7 @@
 
     g = grad[...]
     scal_send(0, 0, 0, jnp.broadcast_to(fold(g * g), (8, 128)))
-    gather_start(0)
+    gather_start(0, g.astype(BF))
 
     send(
         frames.at[share(kept_from, core)], x.at[share(kept, core)], xs_sem.at[0], xr_sem.at[0], across
@@ -192,36 +202,36 @@
     loads[0].wait()
     norm_chunk(0)
     norm_chunk(1)
+    gather_forward(0, 1)
+    gather_forward(0, 7)
+    gather_turn(0)
     loads[1].wait()
     norm_chunk(kept)
-    scal_send(0, 1, 1, scal_take(0, 0, 0))
-    gather_forward(0, 1)
-    gather_forward(0, 7)
-    landed(x.at[share(taken, core)], xr_sem.at[0], across)
-    send(x.at[share(taken, core)], x.at[share(taken, core)], xs_sem.at[2], xr_sem.at[2], sibling)
+    gather_forward(0, 2)
+    gather_forward(0, 6)
     loads[2].wait()
     slope_chunk(0)
-    gather_forward(0, 2)
-    gather_forward(0, 6)
-    slope_chunk(1)
     gather_forward(0, 3)
     gather_forward(0, 5)
     gather_forward(0, 4)
-    scal_send(0, 2, 2, scal_take(0, 1, 1))
+    landed(x.at[share(taken, core)], xr_sem.at[0], across)
+    send(x.at[share(taken, core)], x.at[share(taken, core)], xs_sem.at[2], xr_sem.at[2], sibling)
+    slope_chunk(1)
     slope_chunk(kept)
-    landed(wrow.at[1], xr_sem.at[1], across)
-    wcol[chunk(taken), :] = weight_column(wrow[1])
     loads[3].wait()
     loads[4].wait()
     for i in range(2):
         wot[i] = wo[i].astype(F32).T.astype(BF)
+    landed(wrow.at[1], xr_sem.at[1], across)
+    wcol[chunk(taken), :] = weight_column(wrow[1])
     landed(x.at[share(taken, 1 - core)], xr_sem.at[2], sibling)
     norm_chunk(taken)
     slope_chunk(taken)
     gather_end(0)
 
-    def tangent(it, t, mat):
+    def tangent(it, t):
         rows = chunk(t)
+        mat = jnp.concatenate([va[it].reshape(D, CA), vb[it].reshape(D, CB)], axis=1)
         q = dot(normed[rows, :], mat)
         hq = (hs[rows, :] * q).astype(BF)
         give[it, t] = dot(hq, wo[1]).astype(BF)
@@ -252,10 +262,10 @@
         gh = dot(gy[it, t], wot[0]) + dot(gyo[it, t], wot[1])
         ga[rows, :] = (hs[rows, :] * gh).astype(BF)
 
-    def curve(it, mat, get_beta):
-        tangent(it, ORDER[0], mat)
+    def curve(it, get_beta):
+        tangent(it, ORDER[0])
         for i in range(1, NT):
-            tangent(it, ORDER[i], mat)
+            tangent(it, ORDER[i])
             pair_sum(it, ORDER[i - 1])
         pair_sum(it, ORDER[NT - 1])
         beta = get_beta()
@@ -265,23 +275,25 @@
             pull_back(it, ORDER[i - 1])
         scal_send(2 * it + 1, 0, 3, jnp.broadcast_to(energy, (8, 128)))
         pull_back(it, ORDER[NT - 1])
-        scal_send(2 * it + 1, 1, 1, scal_take(2 * it + 1, 0, 3))
 
     def terms(it):
         for off in FAR:
             to = lax.rem(z + off, NZ)
-            block = dot(normed_t[pl.ds(pl.multiple_of(to * BLK, BLK), BLK), :], ga[...])
-            term[it, to] = block.astype(BF).reshape(NW, ROWS, F)
+            block = dot(normed_t[pl.ds(pl.multiple_of(to * BLK, BLK), BLK), :], ga[...]).astype(BF)
+            ta[it, to] = block[:, :CA].reshape(NW, ROWS, CA)
+            tb[it, to] = block[:, CA:].reshape(NW, ROWS, CB)
+            if off:
+                send(tb.at[it, to], bz.at[it, off], cbs_sem.at[it, 0], cbr_sem.at[it, 0], zpeer(off))
             for k in range(1, NW):
                 send(
-                    term.at[it, to, lax.rem(w + k, NW)], fromw.at[it, off, k],
+                    ta.at[it, to, lax.rem(w + k, NW)], fromw.at[it, off, k],
                     ts_sem.at[it], tr_sem.at[it, off], wpeer(k),
                 )
 
     def reduce_block(it, off):
         to = lax.rem(z + off, NZ)
         landed(fromw.at[it, off, pl.ds(1, NW - 1)], tr_sem.at[it, off], wpeer(1))
-        total = term[it, to, w].astype(F32)
+        total = ta[it, to, w].astype(F32)
         for k in range(1, NW):
             total = total + fromw[it, off, k].astype(F32)
         if off:
@@ -289,39 +301,58 @@
             send(toz.at[it, off], fromz.at[it, off], us_sem.at[it], ur_sem.at[it], zpeer(off))
         return total
 
+    def reduce_turn(it):
+        landed(bz.at[it, pl.ds(1, NZ - 1)], cbr_sem.at[it, 0], zpeer(1))
+        total = tb[it, z].astype(F32)
+        for k in range(1, NZ):
+            total = total + bz[it, k].astype(F32)
+        tow[it] = total.astype(BF)
+        for k in range(1, NW):
+            send(tow.at[it, lax.rem(w + k, NW)], bw.at[it, k], cbs_sem.at[it, 1], cbr_sem.at[it, 1], wpeer(k))
+
     def reduce_end(it, total):
+        landed(bw.at[it, pl.ds(1, NW - 1)], cbr_sem.at[it, 1], wpeer(1))
+        total_b = tow[it, w].astype(F32)
+        for k in range(1, NW):
+            total_b = total_b + bw[it, k].astype(F32)
         landed(fromz.at[it, pl.ds(1, NZ - 1)], ur_sem.at[it], zpeer(1))
         for k in range(1, NZ):
             total = total + fromz[it, k].astype(F32)
-        return total
-
-    def reduce(it):
+        return jnp.concatenate([total, total_b], axis=1)
+
+    def reduce(it, extra):
+        pair = scal_take(2 * it + 1, 0, 3)
+        if extra is not None:
+            pair = jnp.concatenate([pair[0:1], extra[0:1], pair[2:8]], axis=0)
+        scal_send(2 * it + 1, 1, 1, pair)
         terms(it)
         scal_send(2 * it + 1, 2, 2, scal_take(2 * it + 1, 1, 1))
-        for off in FAR:
+        for off in FAR[:5]:
+            reduce_block(it, off)
+        reduce_turn(it)
+        for off in FAR[5:]:
             total = reduce_block(it, off)
         total = reduce_end(it, total)
-        return total, jnp.sum(scal_take(2 * it + 1, 2, 2)[0:1], axis=1, keepdims=True)
-
-    curve(0, v[0].reshape(D, F), lambda: None)
-    gg = jnp.sum(scal_take(0, 2, 2)[0:1], axis=1, keepdims=True)
-    ag, energy0 = reduce(0)
+        return total, jnp.sum(scal_take(2 * it + 1, 2, 2), axis=1, keepdims=True)
+
+    curve(0, lambda: None)
+    ag, sums = reduce(0, scal_take(0, 0, 0))
+    energy0, gg = sums[0:1], sums[1:2]
     alpha0 = gg / (energy0 + DAMPING * gg)
     r1 = g - alpha0 * (ag + DAMPING * g)
-    v[1, z, w] = r1.astype(BF)
-    gather_start(1)
+    gather_start(1, r1.astype(BF))
     scal_send(2, 0, 0, jnp.concatenate([fold(r1 * r1), fold(r1 * g), jnp.zeros((6, 128), F32)], axis=0))
     gather_forward(1, 1)
     gather_forward(1, 7)
+    scal_send(2, 1, 1, scal_take(2, 0, 0))
+    gather_turn(1)
     gather_forward(1, 2)
     gather_forward(1, 6)
     gather_forward(1, 3)
     gather_forward(1, 5)
     gather_forward(1, 4)
-    scal_send(2, 1, 1, scal_take(2, 0, 0))
+    scal_send(2, 2, 2, scal_take(2, 1, 1))
     gather_end(1)
-    scal_send(2, 2, 2, scal_take(2, 1, 1))
-
     norms = []
 
     def get_beta():
@@ -329,24 +360,29 @@
         norms.extend([sums[0:1], sums[1:2], sums[0:1] / gg])
         return norms[2]
 
-    curve(1, v[1].reshape(D, F), get_beta)
+    curve(1, get_beta)
     rr1, rg, beta = norms
-    ad1, energy1 = reduce(1)
+    ad1, sums = reduce(1, None)
+    energy1 = sums[0:1]
     d1 = r1 + beta * g
     alpha1 = rr1 / (energy1 + DAMPING * (rr1 + 2.0 * beta * rg + beta * beta * gg))
     sol[...] = alpha0 * g + alpha1 * d1
     res[...] = r1 - alpha1 * (ad1 + DAMPING * d1)
 
     for it in range(2):
-        sent(v.at[it, 0, pl.ds(0, NZ - 1)], zs_sem.at[it], zpeer(1))
-        sent(v.at[it, pl.ds(0, NW - 1)], ws_sem.at[it], wpeer(1))
+        sent(va.at[it, 0, pl.ds(0, NZ - 1)], zs_sem.at[it], zpeer(1))
+        sent(va.at[it, pl.ds(0, NW - 1)], ws_sem.at[it], wpeer(1))
+        sent(vb.at[it, 0, pl.ds(0, NW - 1)], bs_sem.at[it, 0], wpeer(1))
+        sent(vb.at[it, pl.ds(0, NZ - 1)], bs_sem.at[it, 1], zpeer(1))
+        sent(tb.at[it, pl.ds(0, NZ - 1)], cbs_sem.at[it, 0], zpeer(1))
+        sent(tow.at[it, pl.ds(0, NW - 1)], cbs_sem.at[it, 1], wpeer(1))
         sent(give.at[it], cs_sem.at[it], sibling)
         sent(half.at[it], ls_sem.at[it], beside)
         sent(gy.at[it], gs_sem.at[it], sibling)
-        sent(term.at[it, pl.ds(0, NW - 1)], ts_sem.at[it], wpeer(1))
+        sent(ta.at[it, pl.ds(0, NW - 1)], ts_sem.at[it], wpeer(1))
         sent(toz.at[it, pl.ds(1, NZ - 1)], us_sem.at[it], zpeer(1))
     for a in range(4):
-        for phase, n in enumerate((2 if a % 2 else NM, NW, NZ)):
+        for phase, n in enumerate(((NM,), (2, NW, NZ), (NM, NW, NZ), (2, NW, NZ))[a]):
             sent(sc_in.at[a, phase, pl.ds(1, n - 1)], as_sem.at[a, phase], mpeer(1))
     sent(x.at[share(kept, core)], xs_sem.at[0], across)
     sent(wrow.at[0], xs_sem.at[1], across)
@@ -378,7 +414,8 @@
                 pltpu.VMEM((TOK, F), F32),
                 pltpu.VMEM((TOK, 128), F32),
                 pltpu.VMEM((2, 8, 128), F32),
-                pltpu.VMEM((2, NZ, NW, ROWS, F), BF),
+                pltpu.VMEM((2, NZ, NW, ROWS, CA), BF),
+                pltpu.VMEM((2, NZ, NW, ROWS, CB), BF),
                 pltpu.VMEM((NT, CH, HALF), F32),
                 pltpu.VMEM((NT, CH, HALF), F32),
                 pltpu.VMEM((2, NT, CH, HALF), BF),
@@ -388,10 +425,14 @@
                 pltpu.VMEM((2, NT, CH, HALF), BF),
                 pltpu.VMEM((2, NT, CH, HALF), BF),
                 pltpu.VMEM((TOK, F), BF),
-                pltpu.VMEM((2, NZ, NW, ROWS, F), BF),
-                pltpu.VMEM((2, NZ, NW, ROWS, F), BF),
-                pltpu.VMEM((2, NZ, ROWS, F), BF),
-                pltpu.VMEM((2, NZ, ROWS, F), BF),
+                pltpu.VMEM((2, NZ, NW, ROWS, CA), BF),
+                pltpu.VMEM((2, NZ, NW, ROWS, CB), BF),
+                pltpu.VMEM((2, NZ, NW, ROWS, CA), BF),
+                pltpu.VMEM((2, NZ, ROWS, CA), BF),
+                pltpu.VMEM((2, NZ, ROWS, CA), BF),
+                pltpu.VMEM((2, NZ, NW, ROWS, CB), BF),
+                pltpu.VMEM((2, NW, ROWS, CB), BF),
+                pltpu.VMEM((2, NW, ROWS, CB), BF),
                 pltpu.VMEM((4, 3, 8, 128), F32),
                 pltpu.VMEM((4, 3, 8, 8, 128), F32),
                 dma((8,)),
@@ -404,6 +445,8 @@
                 dma((2,)), dma((2,)),
                 dma((4, 3)), dma((4, 3)),
                 dma((3,)), dma((3,)),
+                dma((2, 2)), dma((2, 2)),
+                dma((2, 2)), dma((2, 2)),
             ],
             compiler_params=pltpu.CompilerParams(
                 collective_id=0, has_side_effects=True, vmem_limit_bytes=63 << 20

time: 115 us -> 97.3 us (0.85)
  Pallas kernels: 112 us -> 94.5 us
    pallas_call x1, Pallas kernels: 112 us -> 94.5 us  [on_device(): pl.pallas_call(kernel, out_shape=(out, out), in_specs=[hbm, hbm, hbm, hbm...]
where the time goes in v4:
time: 97.3 us; the launch traced here: 97.1 us
  Pallas kernels  94.5 us (97%)
  local copies, waits for them, and re-layouts  2 us (2%)
    pallas_call x1, Pallas kernels, on_device(): pl.pallas_call(kernel, out_shape=(out, out), in_specs=[hbm, hbm, hbm, hbm...  94.5 us
    unnamed x4, local copies, waits for them, and re-layouts  2 us

profile of v4, /device:TPU:1, one launch (start us, length us, event | category | flops | bytes accessed | tf_op | source)
XLA Modules:
  0.0 97.1 jit_solution(269380518966685323)
XLA Ops:
  0.6 94.5 %shard_map.86 = (f32[16,512]{1,0:T(8,128)}, f32[16,512]{1,0:T(8,128)}) custom-call(bf16[512,1024]{1,0:T(8,128)(2,1)} %frames.1, f32[1,1024]{1,0:T(1,128)} %bitcast.2, bf16[1024,512]{1,0:T(8,128)(2,1)} %w_inner.1, bf16[512,1024]{1,0:T(8,128)(2,1)} %w_outer.1, s32[1,8]{1,0:T(1,128)} %lengths.1, s32[4,128]{1,0:T(4,128)} %bitcast.3, f32[16,512]{1,0:T(8,128)} %grad_in.1), custom_call_target="tpu_custom_call" | custom-call | flops 4831838208 | bytes 4194304 | tf_op jit(solution)/shard_map/pallas_call | solution.py:399
  95.1 0.0 copy-start
  95.1 1.4 %copy.11 = f32[16,512]{1,0:T(8,128)} copy(f32[16,512]{1,0:T(8,128)} %get-tuple-element.4) | data formatting | bytes 65536
  96.5 0.0 copy-done
  96.5 0.6 copy.12
Async XLA Ops:
  95.1 1.4 %copy-start = (f32[16,512]{1,0:T(8,128)S(1)}, f32[16,512]{1,0:T(8,128)}, u32[]{:S(2)}) copy-start(f32[16,512]{1,0:T(8,128)} %get-tuple-element.5) | copy-start | bytes 98308

commit v5 on v4

--- a/solution.py
+++ b/solution.py
@@ -18,6 +18,7 @@
 BF, F32 = jnp.bfloat16, jnp.float32
 NEAR = (1, 7, 2, 6, 3, 5, 4)
 FAR = (4, 3, 5, 2, 6, 1, 7, 0)
+WFAR = (3, 5, 7, 1, 4, 2, 6)
 ORDER = (0, 2, 1, 3)
 
 
@@ -31,7 +32,7 @@
 
 
 def kernel(
-    frames, gain_in, w_inner, w_outer, lengths, mask_in, grad_in, sol, res,
+    frames, gain_in, w_inner, w_outer, lengths, mask_in, grad_in, out,
     grad, gain, mask, x, wi, wo, wot, normed, normed_t, hs, wcol,
     wrow, va, vb, u_first, own, give, got, half, theirs, gy, gyo, ga, ta, tb, fromw, toz, fromz, bz, tow, bw, sc_own, sc_in,
     in_sem, zs_sem, zr_sem, ws_sem, wr_sem, cs_sem, cr_sem, ls_sem, lr_sem, gs_sem, gr_sem,
@@ -106,7 +107,7 @@
     pl.semaphore_wait(barrier, NZ + NW + NM - 2)
 
     def gather_pass(it, block):
-        for k in range(1, NW):
+        for k in WFAR:
             send(va.at[it, block, w], va.at[it, block, w], ws_sem.at[it], wr_sem.at[it], wpeer(k))
 
     def gather_start(it, rows):
@@ -114,7 +115,7 @@
         vb[it, z, w] = rows[:, CA:]
         for k in NEAR:
             send(va.at[it, z, w], va.at[it, z, w], zs_sem.at[it], zr_sem.at[it, k], zpeer(k))
-        for k in range(1, NW):
+        for k in WFAR:
             send(vb.at[it, z, w], vb.at[it, z, w], bs_sem.at[it, 0], br_sem.at[it, 0], wpeer(k))
         gather_pass(it, z)
 
@@ -284,7 +285,7 @@
             tb[it, to] = block[:, CA:].reshape(NW, ROWS, CB)
             if off:
                 send(tb.at[it, to], bz.at[it, off], cbs_sem.at[it, 0], cbr_sem.at[it, 0], zpeer(off))
-            for k in range(1, NW):
+            for k in WFAR:
                 send(
                     ta.at[it, to, lax.rem(w + k, NW)], fromw.at[it, off, k],
                     ts_sem.at[it], tr_sem.at[it, off], wpeer(k),
@@ -307,7 +308,7 @@
         for k in range(1, NZ):
             total = total + bz[it, k].astype(F32)
         tow[it] = total.astype(BF)
-        for k in range(1, NW):
+        for k in WFAR:
             send(tow.at[it, lax.rem(w + k, NW)], bw.at[it, k], cbs_sem.at[it, 1], cbr_sem.at[it, 1], wpeer(k))
 
     def reduce_end(it, total):
@@ -366,8 +367,8 @@
     energy1 = sums[0:1]
     d1 = r1 + beta * g
     alpha1 = rr1 / (energy1 + DAMPING * (rr1 + 2.0 * beta * rg + beta * beta * gg))
-    sol[...] = alpha0 * g + alpha1 * d1
-    res[...] = r1 - alpha1 * (ad1 + DAMPING * d1)
+    out[0] = alpha0 * g + alpha1 * d1
+    out[1] = r1 - alpha1 * (ad1 + DAMPING * d1)
 
     for it in range(2):
         sent(va.at[it, 0, pl.ds(0, NZ - 1)], zs_sem.at[it], zpeer(1))
@@ -394,13 +395,12 @@
     vmem = pl.BlockSpec(memory_space=pltpu.VMEM)
     smem = pl.BlockSpec(memory_space=pltpu.SMEM)
     dma = pltpu.SemaphoreType.DMA
-    out = jax.ShapeDtypeStruct((ROWS, F), F32)
-    return tuple(
+    both = (
         pl.pallas_call(
             kernel,
-            out_shape=(out, out),
+            out_shape=jax.ShapeDtypeStruct((2, ROWS, F), F32),
             in_specs=[hbm, hbm, hbm, hbm, smem, hbm, hbm],
-            out_specs=(vmem, vmem),
+            out_specs=vmem,
             scratch_shapes=[
                 pltpu.VMEM((ROWS, F), F32),
                 pltpu.VMEM((1, D), F32),
@@ -456,6 +456,7 @@
             frames, norm_gain.reshape(1, D), w_inner, w_outer, lengths, frame_mask.reshape(NT, CH), gradient,
         )
     )
+    return both[0], both[1]
 
 
 def solution(mesh):

time: 97.3 us -> 96.5 us (level)
    unnamed x4 -> x0, local copies, waits for them, and re-layouts: 2 us -> none
    squeeze x0 -> x1, local copies, waits for them, and re-layouts: none -> 1.41 us  [on_device(): return (both[0], both[1])]
where the time goes in v5:
time: 96.5 us; the launch traced here: 96.3 us
  Pallas kernels  94.3 us (98%)
  local copies, waits for them, and re-layouts  1.41 us (1%)
    pallas_call x1, Pallas kernels, on_device(): pl.pallas_call(kernel, out_shape=jax.ShapeDtypeStruct((2, ROWS, F), F32),...  94.3 us

profile of v5, /device:TPU:1, one launch (start us, length us, event | category | flops | bytes accessed | tf_op | source)
XLA Modules:
  0.0 96.3 jit_solution(1293411693716783997)
XLA Ops:
  0.6 94.3 %shard_map.86 = f32[2,16,512]{2,1,0:T(8,128)} custom-call(bf16[512,1024]{1,0:T(8,128)(2,1)} %frames.1, f32[1,1024]{1,0:T(1,128)} %bitcast.6, bf16[1024,512]{1,0:T(8,128)(2,1)} %w_inner.1, bf16[512,1024]{1,0:T(8,128)(2,1)} %w_outer.1, s32[1,8]{1,0:T(1,128)} %lengths.1, s32[4,128]{1,0:T(4,128)} %bitcast.7, f32[16,512]{1,0:T(8,128)} %grad_in.1), custom_call_target="tpu_custom_call" | custom-call | flops 4831838208 | bytes 4194304 | tf_op jit(solution)/shard_map/pallas_call | solution.py:399
  94.9 1.4 %slice_bitcast_fusion = (f32[16,512]{1,0:T(8,128)}, f32[16,512]{1,0:T(8,128)}) fusion(f32[2,16,512]{2,1,0:T(8,128)} %shard_map.86), kind=kLoop, calls=%fused_computation | loop fusion | bytes 131072 | tf_op jit(solution)/shard_map/squeeze | solution.py:459

commit v6 on v5

--- a/solution.py
+++ b/solution.py
@@ -72,6 +72,11 @@
             src_ref=ref, dst_ref=ref, send_sem=ssem, recv_sem=ssem, device_id=dev, device_id_type=MESH
         ).wait_send()
 
+    barrier = pltpu.get_barrier_semaphore()
+    greeted = [zpeer(k) for k in NEAR[::-1]] + [wpeer(k) for k in WFAR] + [mpeer(k) for k in range(1, NM)] + [across]
+    for device in greeted:
+        pl.semaphore_signal(barrier, inc=1, device_id=device, device_id_type=MESH)
+
     small = [
         pltpu.make_async_copy(grad_in, grad, in_sem.at[4]),
         pltpu.make_async_copy(gain_in, gain, in_sem.at[5]),
@@ -94,25 +99,21 @@
     ]
     for c in loads:
         c.start()
-    barrier = pltpu.get_barrier_semaphore()
-    for k in range(1, NZ):
-        pl.semaphore_signal(barrier, inc=1, device_id=zpeer(k), device_id_type=MESH)
-    for k in range(1, NW):
-        pl.semaphore_signal(barrier, inc=1, device_id=wpeer(k), device_id_type=MESH)
-    for k in range(1, NM):
-        pl.semaphore_signal(barrier, inc=1, device_id=mpeer(k), device_id_type=MESH)
-    pl.semaphore_signal(barrier, inc=1, device_id=across, device_id_type=MESH)
+    def gather_own(it, rows):
+        va[it, z, w] = rows[:, :CA]
+        vb[it, z, w] = rows[:, CA:]
+
     for c in small:
         c.wait()
-    pl.semaphore_wait(barrier, NZ + NW + NM - 2)
+    g = grad[...]
+    gather_own(0, g.astype(BF))
+    pl.semaphore_wait(barrier, len(greeted))
 
     def gather_pass(it, block):
         for k in WFAR:
             send(va.at[it, block, w], va.at[it, block, w], ws_sem.at[it], wr_sem.at[it], wpeer(k))
 
-    def gather_start(it, rows):
-        va[it, z, w] = rows[:, :CA]
-        vb[it, z, w] = rows[:, CA:]
+    def gather_start(it):
         for k in NEAR:
             send(va.at[it, z, w], va.at[it, z, w], zs_sem.at[it], zr_sem.at[it, k], zpeer(k))
         for k in WFAR:
@@ -149,9 +150,8 @@
             tile = tile + sc_in[a, phase, k]
         return tile
 
-    g = grad[...]
+    gather_start(0)
     scal_send(0, 0, 0, jnp.broadcast_to(fold(g * g), (8, 128)))
-    gather_start(0, g.astype(BF))
 
     send(
         frames.at[share(kept_from, core)], x.at[share(kept, core)], xs_sem.at[0], xr_sem.at[0], across
@@ -341,7 +341,8 @@
     energy0, gg = sums[0:1], sums[1:2]
     alpha0 = gg / (energy0 + DAMPING * gg)
     r1 = g - alpha0 * (ag + DAMPING * g)
-    gather_start(1, r1.astype(BF))
+    gather_own(1, r1.astype(BF))
+    gather_start(1)
     scal_send(2, 0, 0, jnp.concatenate([fold(r1 * r1), fold(r1 * g), jnp.zeros((6, 128), F32)], axis=0))
     gather_forward(1, 1)
     gather_forward(1, 7)

time: 96.5 us -> 96.5 us (level)
  no operation moved by 1% of the time
where the time goes in v6:
time: 96.5 us; the launch traced here: 96.3 us
  Pallas kernels  94.3 us (98%)
  local copies, waits for them, and re-layouts  1.41 us (1%)
    pallas_call x1, Pallas kernels, on_device(): pl.pallas_call(kernel, out_shape=jax.ShapeDtypeStruct((2, ROWS, F), F32),...  94.3 us

profile of v6, /device:TPU:1, one launch (start us, length us, event | category | flops | bytes accessed | tf_op | source)
XLA Modules:
  0.0 96.3 jit_solution(16141543294102630140)
XLA Ops:
  0.6 94.3 %shard_map.86 = f32[2,16,512]{2,1,0:T(8,128)} custom-call(bf16[512,1024]{1,0:T(8,128)(2,1)} %frames.1, f32[1,1024]{1,0:T(1,128)} %bitcast.6, bf16[1024,512]{1,0:T(8,128)(2,1)} %w_inner.1, bf16[512,1024]{1,0:T(8,128)(2,1)} %w_outer.1, s32[1,8]{1,0:T(1,128)} %lengths.1, s32[4,128]{1,0:T(4,128)} %bitcast.7, f32[16,512]{1,0:T(8,128)} %grad_in.1), custom_call_target="tpu_custom_call" | custom-call | flops 4831838208 | bytes 4194304 | tf_op jit(solution)/shard_map/pallas_call | solution.py:400
  94.9 1.4 %slice_bitcast_fusion = (f32[16,512]{1,0:T(8,128)}, f32[16,512]{1,0:T(8,128)}) fusion(f32[2,16,512]{2,1,0:T(8,128)} %shard_map.86), kind=kLoop, calls=%fused_computation | loop fusion | bytes 131072 | tf_op jit(solution)/shard_map/squeeze | solution.py:460

commit v7 on v5

--- a/solution.py
+++ b/solution.py
@@ -328,10 +328,10 @@
         scal_send(2 * it + 1, 1, 1, pair)
         terms(it)
         scal_send(2 * it + 1, 2, 2, scal_take(2 * it + 1, 1, 1))
-        for off in FAR[:5]:
+        for off in FAR[:3]:
             reduce_block(it, off)
         reduce_turn(it)
-        for off in FAR[5:]:
+        for off in FAR[3:]:
             total = reduce_block(it, off)
         total = reduce_end(it, total)
         return total, jnp.sum(scal_take(2 * it + 1, 2, 2), axis=1, keepdims=True)

time: 96.5 us -> 96.3 us (level)
  no operation moved by 1% of the time
where the time goes in v7:
time: 96.3 us; the launch traced here: 96.1 us
  Pallas kernels  94 us (98%)
  local copies, waits for them, and re-layouts  1.41 us (1%)
    pallas_call x1, Pallas kernels, on_device(): pl.pallas_call(kernel, out_shape=jax.ShapeDtypeStruct((2, ROWS, F), F32),...  94 us

profile of v7, /device:TPU:1, one launch (start us, length us, event | category | flops | bytes accessed | tf_op | source)
XLA Modules:
  0.0 96.1 jit_solution(10679828805828284670)
XLA Ops:
  0.6 94.0 %shard_map.86 = f32[2,16,512]{2,1,0:T(8,128)} custom-call(bf16[512,1024]{1,0:T(8,128)(2,1)} %frames.1, f32[1,1024]{1,0:T(1,128)} %bitcast.6, bf16[1024,512]{1,0:T(8,128)(2,1)} %w_inner.1, bf16[512,1024]{1,0:T(8,128)(2,1)} %w_outer.1, s32[1,8]{1,0:T(1,128)} %lengths.1, s32[4,128]{1,0:T(4,128)} %bitcast.7, f32[16,512]{1,0:T(8,128)} %grad_in.1), custom_call_target="tpu_custom_call" | custom-call | flops 4831838208 | bytes 4194304 | tf_op jit(solution)/shard_map/pallas_call | solution.py:399
  94.7 1.4 %slice_bitcast_fusion = (f32[16,512]{1,0:T(8,128)}, f32[16,512]{1,0:T(8,128)}) fusion(f32[2,16,512]{2,1,0:T(8,128)} %shard_map.86), kind=kLoop, calls=%fused_computation | loop fusion | bytes 131072 | tf_op jit(solution)/shard_map/squeeze | solution.py:459

commit v8 on v5

--- a/solution.py
+++ b/solution.py
@@ -34,7 +34,7 @@
 def kernel(
     frames, gain_in, w_inner, w_outer, lengths, mask_in, grad_in, out,
     grad, gain, mask, x, wi, wo, wot, normed, normed_t, hs, wcol,
-    wrow, va, vb, u_first, own, give, got, half, theirs, gy, gyo, ga, ta, tb, fromw, toz, fromz, bz, tow, bw, sc_own, sc_in,
+    wrow, va, vb, hq, u_first, own, give, got, half, theirs, gy, gyo, ga, ta, tb, fromw, toz, fromz, bz, tow, bw, sc_own, sc_in,
     in_sem, zs_sem, zr_sem, ws_sem, wr_sem, cs_sem, cr_sem, ls_sem, lr_sem, gs_sem, gr_sem,
     ts_sem, tr_sem, us_sem, ur_sem, as_sem, ar_sem, xs_sem, xr_sem, bs_sem, br_sem, cbs_sem, cbr_sem,
 ):
@@ -230,14 +230,15 @@
     slope_chunk(taken)
     gather_end(0)
 
+    def project(it, rows):
+        mat = jnp.concatenate([va[it].reshape(D, CA), vb[it].reshape(D, CB)], axis=1)
+        hq[rows, :] = (hs[rows, :] * dot(normed[rows, :], mat)).astype(BF)
+
     def tangent(it, t):
         rows = chunk(t)
-        mat = jnp.concatenate([va[it].reshape(D, CA), vb[it].reshape(D, CB)], axis=1)
-        q = dot(normed[rows, :], mat)
-        hq = (hs[rows, :] * q).astype(BF)
-        give[it, t] = dot(hq, wo[1]).astype(BF)
+        give[it, t] = dot(hq[rows, :], wo[1]).astype(BF)
         send(give.at[it, t], got.at[it, t], cs_sem.at[it], cr_sem.at[it, t], sibling)
-        own[t] = dot(hq, wo[0])
+        own[t] = dot(hq[rows, :], wo[0])
 
     def pair_sum(it, t):
         landed(got.at[it, t], cr_sem.at[it, t], sibling)
@@ -264,10 +265,15 @@
         ga[rows, :] = (hs[rows, :] * gh).astype(BF)
 
     def curve(it, get_beta):
-        tangent(it, ORDER[0])
-        for i in range(1, NT):
-            tangent(it, ORDER[i])
-            pair_sum(it, ORDER[i - 1])
+        project(it, pl.ds(0, 2 * CH))
+        tangent(it, 0)
+        project(it, pl.ds(2 * CH, 2 * CH))
+        tangent(it, 2)
+        pair_sum(it, 0)
+        tangent(it, 1)
+        pair_sum(it, 2)
+        tangent(it, 3)
+        pair_sum(it, 1)
         pair_sum(it, ORDER[NT - 1])
         beta = get_beta()
         energy = weigh(it, ORDER[0], beta)
@@ -416,6 +422,7 @@
                 pltpu.VMEM((2, 8, 128), F32),
                 pltpu.VMEM((2, NZ, NW, ROWS, CA), BF),
                 pltpu.VMEM((2, NZ, NW, ROWS, CB), BF),
+                pltpu.VMEM((TOK, F), BF),
                 pltpu.VMEM((NT, CH, HALF), F32),
                 pltpu.VMEM((NT, CH, HALF), F32),
                 pltpu.VMEM((2, NT, CH, HALF), BF),

time: 96.5 us -> 96.6 us (level)
  no operation moved by 1% of the time
where the time goes in v8:
time: 96.6 us; the launch traced here: 96.5 us
  Pallas kernels  94.4 us (98%)
  local copies, waits for them, and re-layouts  1.41 us (1%)
    pallas_call x1, Pallas kernels, on_device(): pl.pallas_call(kernel, out_shape=jax.ShapeDtypeStruct((2, ROWS, F), F32),...  94.4 us

profile of v8, /device:TPU:1, one launch (start us, length us, event | category | flops | bytes accessed | tf_op | source)
XLA Modules:
  0.0 96.5 jit_solution(9442433842719468657)
XLA Ops:
  0.6 94.4 %shard_map.86 = f32[2,16,512]{2,1,0:T(8,128)} custom-call(bf16[512,1024]{1,0:T(8,128)(2,1)} %frames.1, f32[1,1024]{1,0:T(1,128)} %bitcast.6, bf16[1024,512]{1,0:T(8,128)(2,1)} %w_inner.1, bf16[512,1024]{1,0:T(8,128)(2,1)} %w_outer.1, s32[1,8]{1,0:T(1,128)} %lengths.1, s32[4,128]{1,0:T(4,128)} %bitcast.7, f32[16,512]{1,0:T(8,128)} %grad_in.1), custom_call_target="tpu_custom_call" | custom-call | flops 4831838208 | bytes 4194304 | tf_op jit(solution)/shard_map/pallas_call | solution.py:405
  95.0 1.4 %slice_bitcast_fusion = (f32[16,512]{1,0:T(8,128)}, f32[16,512]{1,0:T(8,128)}) fusion(f32[2,16,512]{2,1,0:T(8,128)} %shard_map.86), kind=kLoop, calls=%fused_computation | loop fusion | bytes 131072 | tf_op jit(solution)/shard_map/squeeze | solution.py:466
